TPU v7x, 32 devices: a whole 2x2x4 slice. The times are simulated.
32 devices in a mesh: ctx: 32 (over z, y, x, core), head: 1.
Axes of the slice: x: 2, y: 2, z: 4, core: 2. Of those that a mesh axis runs over, the one named last changes fastest.
Arguments:
- queries: bfloat16 [16384, 4096], P('ctx', 'head'), may hold values from -8 to 8
- keys: bfloat16 [16384, 1024], P('ctx', 'head'), may hold values from -6 to 6
- values: bfloat16 [16384, 1024], P('ctx', 'head'), may hold values from -6 to 6
- vertical_blocks: int32 [8, 8], P('head'), may hold values from 0 to 127, as said below
- slash_offsets: int32 [8, 8], P('head'), may hold values from 0 to 16, as said below
- out_weight: bfloat16 [4096, 4096], P(None, 'head'), may hold values from -0.5 to 0.5
Outputs:
- output: bfloat16 [16384, 4096], P('ctx', 'head')
Inputs may be any that keep to these rules, and one draw needn't show every extreme that they name: `vertical_blocks`: within each key-value head the 8 entries are distinct; every head lists block 0, and head 0 lists block 127. `slash_offsets`: within each key-value head the 8 offsets are distinct, and every head holds 0 and 16.
All inputs are finite; a program needn't handle non-finite values.
Results may differ from a plain program's by a relative error of at most 0.0057.
Values may be sent and summed in bfloat16 or wider, within the bound.
No kernel may reach another device: no remote copies, remote signals or barrier semaphores. Data moves between devices by JAX's collectives and lax.ppermute only.
A program may use at most 192 MiB of HBM per device.

v0:
```python
import math

import jax
import jax.numpy as jnp
from jax import lax
from jax.sharding import PartitionSpec as P

HD = 128
BLK = 128
MAXOFF = 16


def from_behind(value, axis, by):
    size = lax.axis_size(axis)
    pairs = [(i, i + by) for i in range(size) if 0 <= i + by < size]
    return lax.ppermute(value, axis, pairs)


def select_slots(onehot, stacked):
    return jnp.einsum("ejs,xesbh->xejbh", onehot, stacked, preferred_element_type=jnp.float32)


def body(queries, keys, values, vertical_blocks, slash_offsets, out_weight):
    tokens_dev = queries.shape[0]
    kv_heads = keys.shape[1] // HD
    group_size = queries.shape[1] // keys.shape[1]
    local_blocks = tokens_dev // BLK
    reach = MAXOFF // local_blocks
    ctx_pos = lax.axis_index("ctx")
    paired = jnp.stack([keys, values], 0).reshape(2, local_blocks, BLK, kv_heads, HD)
    pieces = [paired]
    for distance in range(1, reach + 1):
        pieces.insert(0, from_behind(paired, "ctx", distance))
    window = jnp.concatenate(pieces, 1).transpose(0, 3, 1, 2, 4)
    by_head = paired.transpose(0, 3, 1, 2, 4)
    owner = vertical_blocks // local_blocks
    within = vertical_blocks % local_blocks
    onehot = (
        within[:, :, None] == jnp.arange(local_blocks, dtype=jnp.int32)[None, None, :]
    ).astype(jnp.bfloat16)
    candidate = select_slots(onehot, by_head)
    masked = jnp.where((owner == ctx_pos)[None, :, :, None, None], candidate, 0.0)
    vertical_kv = lax.psum(masked, "ctx").astype(jnp.bfloat16)
    score_scale = 1.0 / math.sqrt(HD)
    positions = jnp.arange(BLK, dtype=jnp.int32)
    causal = positions[None, :] <= positions[:, None]

    def pick_blocks(heads, picks):
        return jnp.take(heads, picks, axis=1)

    def attend(block_idx):
        global_block = ctx_pos * local_blocks + block_idx
        slash_start = global_block - slash_offsets
        window_index = reach * local_blocks + block_idx - slash_offsets
        slash_kv = jax.vmap(pick_blocks, in_axes=(1, 0), out_axes=1)(window, window_index)
        keys_all = jnp.concatenate([slash_kv, vertical_kv], 2)
        repeated = jnp.any(vertical_blocks[:, :, None] == slash_start[:, None, :], 2)
        valid = jnp.concatenate([slash_start >= 0, (vertical_blocks < global_block) & ~repeated], 1)
        diagonal = jnp.concatenate(
            [slash_offsets == 0, jnp.zeros(vertical_blocks.shape, jnp.bool_)], 1
        )
        rows = lax.dynamic_slice_in_dim(queries, block_idx * BLK, BLK, 0).reshape(
            BLK, kv_heads, group_size, HD
        )
        scores = (
            jnp.einsum("rhgd,hjcd->hgrjc", rows, keys_all[0], preferred_element_type=jnp.float32)
            * score_scale
        )
        allowed = valid[:, None, None, :, None] & (
            ~diagonal[:, None, None, :, None] | causal[None, None, :, None, :]
        )
        scores = jnp.where(allowed, scores, -1e30)
        top = jnp.max(scores, axis=(3, 4), keepdims=True)
        expo = jnp.exp(scores - top)
        total = jnp.sum(expo, axis=(3, 4), keepdims=True)
        weights = (expo / total).astype(jnp.bfloat16)
        return jnp.einsum(
            "hgrjc,hjcd->rhgd", weights, keys_all[1], preferred_element_type=jnp.float32
        ).astype(jnp.bfloat16)

    attended = lax.map(attend, jnp.arange(local_blocks, dtype=jnp.int32)).reshape(
        tokens_dev, queries.shape[1]
    )
    output = jnp.dot(
        lax.all_gather(attended, "head", axis=1, tiled=True),
        out_weight,
        preferred_element_type=jnp.float32,
    )
    return output.astype(jnp.bfloat16)


def solution(mesh):
    placed = (
        P("ctx", "head"),
        P("ctx", "head"),
        P("ctx", "head"),
        P("head", None),
        P("head", None),
        P(None, "head"),
    )
    return jax.shard_map(
        body, mesh=mesh, in_specs=placed, out_specs=P("ctx", "head"), check_vma=False
    )
```

profile of v0, /device:TPU:25, one launch (start us, length us, event | category | flops | bytes accessed | tf_op | source)
XLA Modules:
  0.0 683.1 jit_solution(12262134522663243180)
XLA Ops:
  14.9 4.5 select_bitcast_fusion.1
  19.4 296.0 %all-reduce.2 = bf16[2,8,8,128,128]{4,2,3,0,1:T(8,128)(2,1)} all-reduce(f32[2,8,8,128,128]{4,2,3,0,1:T(8,128)} %select_bitcast_fusion.1), channel_id=1, replica_groups=mesh['ctx'=32,'head'=1] {'ctx'}, use_global_device_ids=true, to_apply=%region_0.1 | all-reduce | flops 2097152 | bytes 12582912 | tf_op jit(solution)/shard_map/psum | solution.py:43
  315.4 5.5 copy.29
  320.9 48.2 %concatenate.17 = bf16[2,20,128,8,128]{4,1,2,0,3:T(8,128)(2,1)} concatenate(bf16[2,4,128,8,128]{4,1,2,0,3:T(4,128)(2,1)} %collective-permute-done, bf16[2,4,128,8,128]{4,1,2,0,3:T(4,128)(2,1)} %collective-permute-done.1, bf16[2,4,128,8,128]{4,1,2,0,3:T(4,128)(2,1)} %collective-permute-done.2, bf16[2,4,128,8,128]{4,1,2,0,3:T(4,128)(2,1)} %collective-permute-done.3, ...), dimensions={1} | concatenate | bytes 20971520 | tf_op jit(solution)/shard_map/concatenate | solution.py:34
  369.2 9.5 %copy.28 = bf16[2,8,20,128,128]{4,3,2,1,0:T(8,128)(2,1)} copy(bf16[2,8,20,128,128]{4,2,3,0,1:T(8,128)(2,1)} %bitcast.110) | data formatting | bytes 20971520
  378.7 273.0 %while.13 = (s32[]{:T(128)}, bf16[4,128,8,4,128]{4,3,2,1,0:T(4,128)(2,1)}, s32[4]{0:T(128)S(1)}, s32[8,8]{1,0:T(8,128)S(1)}, bf16[2,8,20,128,128]{4,3,2,1,0:T(8,...) while((s32[]{:T(128)}, ...), condition=%wide.region_5.6_spmd.clone, body=%wide.region_1.5_spmd.clone.sunk | while | flops 4419234304 | bytes 161600112 | solution.py:81
  382.9 7.0 %gather_fusion = bf16[64,2,128,128]{3,2,1,0:T(8,128)(2,1)} fusion(bf16[8,2,20,128,128]{4,3,2,0,1:T(8,128)(2,1)} %bitcast.109, s32[64]{0:T(128)S(1)} %reshape.83), kind=kCustom, calls=%fused_computation.clone.clone.1 | custom fusion | bytes 8389120 | tf_op jit(solution)/shard_map/while/body/eval_jaxpr/vmap(jit(_take))/gather | solution.py:49
  399.6 14.6 %fusion.43 = (f32[8,4,128]{2,1,0:T(4,128)S(1)}, f32[8,16,128,128,4]{3,2,4,1,0:T(8,128)}) fusion(pred[8,128,16,128]{1,3,2,0:T(8,128)(4,1)S(1)} %or_and_fusion.2, bf16[128,8,4,128,1]{0,3,2,4,1:T(8,128)(2,1)S(1)} %bitcast.108, bf16[2,8,8,128,128]{4,3,2,1,0:T(8,128)(2,1)} %get-tuple-element.299, bf16[2,8,8,128,128]{4,3,2,1,0:T(8,128)(2,1)} %select_bitcast_fusion.3), kind=kOutput, calls=%fused_computation.6.clone.1 | convolution fusion | flops 2181033984 | bytes 45105152 | tf_op jit(solution)/shard_map/while/body/eval_jaxpr/rhgd,hjcd->hgrjc/dot_general | solution.py:66
  414.2 14.3 %fusion.44 = f32[8,4,128]{2,1,0:T(4,128)S(1)} fusion(f32[8,16,128,128,4]{3,2,4,1,0:T(8,128)} %get-tuple-element.264, f32[8,4,128]{2,1,0:T(4,128)S(1)} %get-tuple-element.265, pred[8,128,16,128]{1,3,2,0:T(8,128)(4,1)S(1)} %or_and_fusion.2), kind=kLoop, calls=%fused_computation.5.clone.1 | loop fusion | flops 33550336 | bytes 35684352 | tf_op jit(solution)/shard_map/while/body/eval_jaxpr/reduce_sum | solution.py:75
  428.5 16.2 %fusion.45 = bf16[1,128,8,4,128]{1,4,3,2,0:T(8,128)(2,1)S(1)} fusion(f32[8,16,128,128,4]{3,2,4,1,0:T(8,128)} %get-tuple-element.264, f32[8,4,128]{2,1,0:T(4,128)S(1)} %fusion.44, f32[8,4,128]{2,1,0:T(4,128)S(1)} %get-tuple-element.265, pred[8,128,16,128]{1,3,2,0:T(8,128)(4,1)S(1)} %or_and_fusion.2, ...), kind=kOutput, calls=%fused_computation.19.clone.1 | convolution fusion | flops 2198339584 | bytes 45121536 | tf_op jit(solution)/shard_map/while/body/eval_jaxpr/hgrjc,hjcd->rhgd/dot_general | solution.py:77
  451.2 7.0 %gather_fusion = bf16[64,2,128,128]{3,2,1,0:T(8,128)(2,1)} fusion(bf16[8,2,20,128,128]{4,3,2,0,1:T(8,128)(2,1)} %bitcast.109, s32[64]{0:T(128)S(1)} %reshape.83), kind=kCustom, calls=%fused_computation.clone.clone.1 | custom fusion | bytes 8389120 | tf_op jit(solution)/shard_map/while/body/eval_jaxpr/vmap(jit(_take))/gather | solution.py:49
  467.8 14.6 %fusion.43 = (f32[8,4,128]{2,1,0:T(4,128)S(1)}, f32[8,16,128,128,4]{3,2,4,1,0:T(8,128)}) fusion(pred[8,128,16,128]{1,3,2,0:T(8,128)(4,1)S(1)} %or_and_fusion.2, bf16[128,8,4,128,1]{0,3,2,4,1:T(8,128)(2,1)S(1)} %bitcast.108, bf16[2,8,8,128,128]{4,3,2,1,0:T(8,128)(2,1)} %get-tuple-element.299, bf16[2,8,8,128,128]{4,3,2,1,0:T(8,128)(2,1)} %select_bitcast_fusion.3), kind=kOutput, calls=%fused_computation.6.clone.1 | convolution fusion | flops 2181033984 | bytes 45105152 | tf_op jit(solution)/shard_map/while/body/eval_jaxpr/rhgd,hjcd->hgrjc/dot_general | solution.py:66
  482.4 14.3 %fusion.44 = f32[8,4,128]{2,1,0:T(4,128)S(1)} fusion(f32[8,16,128,128,4]{3,2,4,1,0:T(8,128)} %get-tuple-element.264, f32[8,4,128]{2,1,0:T(4,128)S(1)} %get-tuple-element.265, pred[8,128,16,128]{1,3,2,0:T(8,128)(4,1)S(1)} %or_and_fusion.2), kind=kLoop, calls=%fused_computation.5.clone.1 | loop fusion | flops 33550336 | bytes 35684352 | tf_op jit(solution)/shard_map/while/body/eval_jaxpr/reduce_sum | solution.py:75
  496.7 16.2 %fusion.45 = bf16[1,128,8,4,128]{1,4,3,2,0:T(8,128)(2,1)S(1)} fusion(f32[8,16,128,128,4]{3,2,4,1,0:T(8,128)} %get-tuple-element.264, f32[8,4,128]{2,1,0:T(4,128)S(1)} %fusion.44, f32[8,4,128]{2,1,0:T(4,128)S(1)} %get-tuple-element.265, pred[8,128,16,128]{1,3,2,0:T(8,128)(4,1)S(1)} %or_and_fusion.2, ...), kind=kOutput, calls=%fused_computation.19.clone.1 | convolution fusion | flops 2198339584 | bytes 45121536 | tf_op jit(solution)/shard_map/while/body/eval_jaxpr/hgrjc,hjcd->rhgd/dot_general | solution.py:77
  519.4 7.0 %gather_fusion = bf16[64,2,128,128]{3,2,1,0:T(8,128)(2,1)} fusion(bf16[8,2,20,128,128]{4,3,2,0,1:T(8,128)(2,1)} %bitcast.109, s32[64]{0:T(128)S(1)} %reshape.83), kind=kCustom, calls=%fused_computation.clone.clone.1 | custom fusion | bytes 8389120 | tf_op jit(solution)/shard_map/while/body/eval_jaxpr/vmap(jit(_take))/gather | solution.py:49
  536.1 14.6 %fusion.43 = (f32[8,4,128]{2,1,0:T(4,128)S(1)}, f32[8,16,128,128,4]{3,2,4,1,0:T(8,128)}) fusion(pred[8,128,16,128]{1,3,2,0:T(8,128)(4,1)S(1)} %or_and_fusion.2, bf16[128,8,4,128,1]{0,3,2,4,1:T(8,128)(2,1)S(1)} %bitcast.108, bf16[2,8,8,128,128]{4,3,2,1,0:T(8,128)(2,1)} %get-tuple-element.299, bf16[2,8,8,128,128]{4,3,2,1,0:T(8,128)(2,1)} %select_bitcast_fusion.3), kind=kOutput, calls=%fused_computation.6.clone.1 | convolution fusion | flops 2181033984 | bytes 45105152 | tf_op jit(solution)/shard_map/while/body/eval_jaxpr/rhgd,hjcd->hgrjc/dot_general | solution.py:66
  550.7 14.3 %fusion.44 = f32[8,4,128]{2,1,0:T(4,128)S(1)} fusion(f32[8,16,128,128,4]{3,2,4,1,0:T(8,128)} %get-tuple-element.264, f32[8,4,128]{2,1,0:T(4,128)S(1)} %get-tuple-element.265, pred[8,128,16,128]{1,3,2,0:T(8,128)(4,1)S(1)} %or_and_fusion.2), kind=kLoop, calls=%fused_computation.5.clone.1 | loop fusion | flops 33550336 | bytes 35684352 | tf_op jit(solution)/shard_map/while/body/eval_jaxpr/reduce_sum | solution.py:75
  565.0 16.2 %fusion.45 = bf16[1,128,8,4,128]{1,4,3,2,0:T(8,128)(2,1)S(1)} fusion(f32[8,16,128,128,4]{3,2,4,1,0:T(8,128)} %get-tuple-element.264, f32[8,4,128]{2,1,0:T(4,128)S(1)} %fusion.44, f32[8,4,128]{2,1,0:T(4,128)S(1)} %get-tuple-element.265, pred[8,128,16,128]{1,3,2,0:T(8,128)(4,1)S(1)} %or_and_fusion.2, ...), kind=kOutput, calls=%fused_computation.19.clone.1 | convolution fusion | flops 2198339584 | bytes 45121536 | tf_op jit(solution)/shard_map/while/body/eval_jaxpr/hgrjc,hjcd->rhgd/dot_general | solution.py:77
  587.7 7.0 %gather_fusion = bf16[64,2,128,128]{3,2,1,0:T(8,128)(2,1)} fusion(bf16[8,2,20,128,128]{4,3,2,0,1:T(8,128)(2,1)} %bitcast.109, s32[64]{0:T(128)S(1)} %reshape.83), kind=kCustom, calls=%fused_computation.clone.clone.1 | custom fusion | bytes 8389120 | tf_op jit(solution)/shard_map/while/body/eval_jaxpr/vmap(jit(_take))/gather | solution.py:49
  604.3 14.6 %fusion.43 = (f32[8,4,128]{2,1,0:T(4,128)S(1)}, f32[8,16,128,128,4]{3,2,4,1,0:T(8,128)}) fusion(pred[8,128,16,128]{1,3,2,0:T(8,128)(4,1)S(1)} %or_and_fusion.2, bf16[128,8,4,128,1]{0,3,2,4,1:T(8,128)(2,1)S(1)} %bitcast.108, bf16[2,8,8,128,128]{4,3,2,1,0:T(8,128)(2,1)} %get-tuple-element.299, bf16[2,8,8,128,128]{4,3,2,1,0:T(8,128)(2,1)} %select_bitcast_fusion.3), kind=kOutput, calls=%fused_computation.6.clone.1 | convolution fusion | flops 2181033984 | bytes 45105152 | tf_op jit(solution)/shard_map/while/body/eval_jaxpr/rhgd,hjcd->hgrjc/dot_general | solution.py:66
  618.9 14.3 %fusion.44 = f32[8,4,128]{2,1,0:T(4,128)S(1)} fusion(f32[8,16,128,128,4]{3,2,4,1,0:T(8,128)} %get-tuple-element.264, f32[8,4,128]{2,1,0:T(4,128)S(1)} %get-tuple-element.265, pred[8,128,16,128]{1,3,2,0:T(8,128)(4,1)S(1)} %or_and_fusion.2), kind=kLoop, calls=%fused_computation.5.clone.1 | loop fusion | flops 33550336 | bytes 35684352 | tf_op jit(solution)/shard_map/while/body/eval_jaxpr/reduce_sum | solution.py:75
  633.3 16.2 %fusion.45 = bf16[1,128,8,4,128]{1,4,3,2,0:T(8,128)(2,1)S(1)} fusion(f32[8,16,128,128,4]{3,2,4,1,0:T(8,128)} %get-tuple-element.264, f32[8,4,128]{2,1,0:T(4,128)S(1)} %fusion.44, f32[8,4,128]{2,1,0:T(4,128)S(1)} %get-tuple-element.265, pred[8,128,16,128]{1,3,2,0:T(8,128)(4,1)S(1)} %or_and_fusion.2, ...), kind=kOutput, calls=%fused_computation.19.clone.1 | convolution fusion | flops 2198339584 | bytes 45121536 | tf_op jit(solution)/shard_map/while/body/eval_jaxpr/hgrjc,hjcd->rhgd/dot_general | solution.py:77
  651.7 7.8 %reshape.61 = bf16[512,4096]{1,0:T(8,128)(2,1)} reshape(bf16[4,128,8,4,128]{4,3,2,1,0:T(4,128)(2,1)} %get-tuple-element.121) | data formatting | bytes 8388608 | tf_op jit(solution)/shard_map/reshape | solution.py:81
  659.5 23.6 %convolution_convert_fusion = bf16[512,4096]{1,0:T(8,128)(2,1)} fusion(bf16[512,4096]{1,0:T(8,128)(2,1)} %reshape.61, bf16[4096,4096]{1,0:T(8,128)(2,1)} %param.13), kind=kOutput, calls=%fused_computation.41 | convolution fusion | flops 17181966336 | bytes 41943040 | tf_op jit(solution)/shard_map/dot_general | solution.py:84
  (82 shorter events, 71.8 us)
Async XLA Ops:
  0.0 2.4 copy-start
  0.0 14.8 %copy-start.1 = (s32[8,8]{1,0:T(8,128)S(1)}, s32[8,8]{1,0:T(8,128)}, u32[]{:S(2)}) copy-start(s32[8,8]{1,0:T(8,128)} %param.11) | copy-start | bytes 772
  3.6 317.3 %collective-permute-start = (bf16[2,4,128,8,128]{4,1,2,0,3:T(4,128)(2,1)S(1)}, bf16[2,4,128,8,128]{4,1,2,0,3:T(4,128)(2,1)}, u32[]{:S(2)}, u32[]{:S(2)}) collective-permute-start(bf16[2,4,128,8,128]{4,1,2,0,3:T(4,128)(2,1)S(1)} %copy_dynamic-update-slice_fusion), channel_id=1, source_target_pairs={{0,4},{1,5},{2,6},{3,7},{4,8},{5,9},{6,10},{7,11},{8,12},{9,13},{1... | collective-permute-start | bytes 6291464 | tf_op jit(solution)/shard_map/ppermute | solution.py:16
  6.7 314.2 %collective-permute-start.1 = (bf16[2,4,128,8,128]{4,1,2,0,3:T(4,128)(2,1)S(1)}, bf16[2,4,128,8,128]{4,1,2,0,3:T(4,128)(2,1)}, u32[]{:S(2)}, u32[]{:S(2)}) collective-permute-start(bf16[2,4,128,8,128]{4,1,2,0,3:T(4,128)(2,1)S(1)} %copy_dynamic-update-slice_fusion), channel_id=1, source_target_pairs={{0,3},{1,4},{2,5},{3,6},{4,7},{5,8},{6,9},{7,10},{8,11},{9,12},{10... | collective-permute-start | bytes 6291464 | tf_op jit(solution)/shard_map/ppermute | solution.py:16
  8.7 312.2 %collective-permute-start.2 = (bf16[2,4,128,8,128]{4,1,2,0,3:T(4,128)(2,1)S(1)}, bf16[2,4,128,8,128]{4,1,2,0,3:T(4,128)(2,1)}, u32[]{:S(2)}, u32[]{:S(2)}) collective-permute-start(bf16[2,4,128,8,128]{4,1,2,0,3:T(4,128)(2,1)S(1)} %copy_dynamic-update-slice_fusion), channel_id=1, source_target_pairs={{0,2},{1,3},{2,4},{3,5},{4,6},{5,7},{6,8},{7,9},{8,10},{9,11},{10,... | collective-permute-start | bytes 6291464 | tf_op jit(solution)/shard_map/ppermute | solution.py:16
  11.8 309.1 %collective-permute-start.3 = (bf16[2,4,128,8,128]{4,1,2,0,3:T(4,128)(2,1)S(1)}, bf16[2,4,128,8,128]{4,1,2,0,3:T(4,128)(2,1)}, u32[]{:S(2)}, u32[]{:S(2)}) collective-permute-start(bf16[2,4,128,8,128]{4,1,2,0,3:T(4,128)(2,1)S(1)} %copy_dynamic-update-slice_fusion), channel_id=1, source_target_pairs={{0,1},{1,2},{2,3},{3,4},{4,5},{5,6},{6,7},{7,8},{8,9},{9,10},{10,1... | collective-permute-start | bytes 6291464 | tf_op jit(solution)/shard_map/ppermute | solution.py:16
  369.2 9.5 %copy-start.2 = (s32[8,8]{1,0:T(8,128)S(1)}, s32[8,8]{1,0:T(8,128)}, u32[]{:S(2)}) copy-start(s32[8,8]{1,0:T(8,128)} %param.12) | copy-start | bytes 772
where the time goes:
time: 687 us; the launch traced here: 683 us
  blocking collectives  296 us (43%)
  matrix products  151 us (22%)
  local copies, waits for them, and re-layouts  141 us (21%)
  other arithmetic  75.9 us (11%)
  starting transfers between devices  11.2 us (2%)
  loops' own time  7.73 us (1%)
    psum x1, blocking collectives, body(): vertical_kv = lax.psum(masked, 'ctx').astype(jnp.bfloat16)  296 us
    dot_general x4, matrix products, attend(): jnp.einsum('hgrjc,hjcd->rhgd', weights, keys_all[1], preferred_element_ty...  64.6 us
    dot_general x4, matrix products, attend(): jnp.einsum('rhgd,hjcd->hgrjc', rows, keys_all[0], preferred_element_type=...  58.4 us
    reduce_sum x4, other arithmetic, attend(): total = jnp.sum(expo, axis=(3, 4), keepdims=True)  57.3 us
    concatenate x1, local copies, waits for them, and re-layouts, body(): window = jnp.concatenate(pieces, 1).transpose(0, 3, 1, 2, 4)  48.2 us
    gather x12, local copies, waits for them, and re-layouts, pick_blocks(): return jnp.take(heads, picks, axis=1)  39.1 us
    dot_general x1, matrix products, body(): jnp.dot(lax.all_gather(attended, 'head', axis=1, tiled=True), out_weight,...  23.6 us
    unnamed x11, local copies, waits for them, and re-layouts  17.7 us
  transfers between devices with their start and end apart: 4, of which 0 were waited for; matrix products, arithmetic and copies ran while one was open for 1% of the time, Pallas kernels for 0%

commit v1 on v0

v1 whole, which is shorter than its diff:
```python
import functools
import math

import jax
import jax.numpy as jnp
from jax import lax
from jax.experimental import pallas as pl
from jax.experimental.pallas import tpu as pltpu
from jax.sharding import PartitionSpec as P

HD = 128
BLK = 128
MAXOFF = 16
MASKED = -1e30
VMEM_LIMIT = 56 * 1024 * 1024


def shifted(value, by, wrap_pairs=None):
    size = lax.axis_size("ctx")
    pairs = wrap_pairs or [(i, i + by) for i in range(size) if 0 <= i + by < size]
    return lax.ppermute(value, "ctx", pairs)


def swapped(value):
    size = lax.axis_size("ctx")
    return lax.ppermute(value, "ctx", [(i, i ^ 1) for i in range(size)])


def pick_kernel(place, k_ref, v_ref, out_ref):
    n_slots = pl.num_programs(1)
    owned = place[1, pl.program_id(0) * n_slots + pl.program_id(1)]
    keep = owned == 1

    @pl.when(keep)
    def _():
        out_ref[:, :HD] = k_ref[...]
        out_ref[:, HD:] = v_ref[...]

    @pl.when(jnp.logical_not(keep))
    def _():
        out_ref[...] = jnp.zeros_like(out_ref)


def pick_vertical(kv_chip, place, heads, slots):
    return pl.pallas_call(
        pick_kernel,
        grid_spec=pltpu.PrefetchScalarGridSpec(
            num_scalar_prefetch=1,
            grid=(heads, slots),
            in_specs=[
                pl.BlockSpec((BLK, HD), lambda e, j, place: (place[0, e * slots + j], e)),
                pl.BlockSpec((BLK, HD), lambda e, j, place: (place[0, e * slots + j], heads + e)),
            ],
            out_specs=pl.BlockSpec((BLK, 2 * HD), lambda e, j, place: (e * slots + j, 0)),
        ),
        out_shape=jax.ShapeDtypeStruct((heads * slots * BLK, 2 * HD), kv_chip.dtype),
        name="pick_vertical",
    )(place, kv_chip, kv_chip)


def attend_kernel(cfg, info, vert, slash, *refs):
    pair, local, group, reach, n_slash, n_vert = cfg
    q_refs, refs = refs[:pair], refs[pair:]
    k_refs, v_refs, refs = refs[: reach + 1], refs[reach + 1 : 2 * reach + 2], refs[2 * reach + 2 :]
    kv_vert, masks, refs = refs[0], refs[1], refs[2:]
    out_refs, refs = refs[:pair], refs[pair:]
    kwin, vwin, kg, vg, qx, sc = refs
    e = pl.program_id(0)
    chip, core = info[0], info[1]
    dev_rows = local * BLK
    chip_blocks = pair * local
    chip_rows = chip_blocks * BLK
    width = (n_slash + n_vert) * BLK
    step = min(2 * BLK, width)
    factor = math.log2(math.e) / math.sqrt(HD)

    for back in range(reach + 1):
        for slot in range(pair):
            owner = core ^ slot if pair > 1 else 0
            at = pl.multiple_of((reach - back) * chip_rows + owner * dev_rows, dev_rows)
            rows = slice(slot * dev_rows, (slot + 1) * dev_rows)
            kwin[pl.ds(at, dev_rows), :] = k_refs[back][rows, :]
            vwin[pl.ds(at, dev_rows), :] = v_refs[back][rows, :]
    kg[n_slash * BLK :, :HD] = kv_vert[:, :HD]
    vg[n_slash * BLK :, :HD] = kv_vert[:, HD:]
    vg[:, HD:] = jnp.ones((width, HD), vg.dtype)
    row = lax.broadcasted_iota(jnp.int32, (BLK, HD), 0)
    col = lax.broadcasted_iota(jnp.int32, (BLK, HD), 1)
    eye = jnp.where(row == col, 1.0, 0.0).astype(qx.dtype)
    for g in range(group):
        qx[g * BLK : (g + 1) * BLK, HD:] = eye

    for slot in range(pair):

        def one_block(b, carry, slot=slot):
            rel = (core ^ slot if pair > 1 else 0) * local + b
            here = chip * chip_blocks + rel
            starts = [here - slash[e, j] for j in range(n_slash)]
            for j in range(n_slash):
                off = slash[e, j]
                src = pl.multiple_of((reach * chip_blocks + rel - off) * BLK, BLK)
                rows = slice(j * BLK, (j + 1) * BLK)
                kg[rows, :HD] = kwin[pl.ds(src, BLK), :]
                vg[rows, :HD] = vwin[pl.ds(src, BLK), :]
                kind = jnp.where(starts[j] < 0, 2, jnp.where(off == 0, 1, 0))
                kg[rows, HD:] = masks[kind]
            for j in range(n_vert):
                block = vert[e, j]
                hidden = block >= here
                for start in starts:
                    hidden = hidden | (block == start)
                rows = slice((n_slash + j) * BLK, (n_slash + j + 1) * BLK)
                kg[rows, HD:] = masks[jnp.where(hidden, 2, 0)]
            q_rows = pl.ds(pl.multiple_of(b * BLK, BLK), BLK)
            for g in range(group):
                qx[g * BLK : (g + 1) * BLK, :HD] = q_refs[slot][q_rows, g * HD : (g + 1) * HD]
            top = None
            for t in range(0, width, step):
                s = lax.dot_general(
                    qx[...], kg[t : t + step, :], (((1,), (1,)), ((), ())),
                    preferred_element_type=jnp.float32,
                )
                sc[:, t : t + step] = s
                for u in range(0, step, HD):
                    piece = s[:, u : u + HD]
                    top = piece if top is None else jnp.maximum(top, piece)
            top = jnp.max(top, axis=1, keepdims=True)
            acc = None
            for t in range(0, width, step):
                p = jnp.exp2((sc[:, t : t + step] - top) * factor).astype(vg.dtype)
                o = jnp.dot(p, vg[t : t + step, :], preferred_element_type=jnp.float32)
                acc = o if acc is None else acc + o
            res = (acc[:, :HD] / acc[:, HD:]).astype(out_refs[slot].dtype)
            for g in range(group):
                out_refs[slot][q_rows, g * HD : (g + 1) * HD] = res[g * BLK : (g + 1) * BLK]
            return carry

        lax.fori_loop(0, local, one_block, 0)


def attend(qs, windows, kv_vert, vert, slash, info, heads, local):
    pair, reach = len(qs), len(windows) - 1
    dev_rows = qs[0].shape[0]
    group = qs[0].shape[1] // (heads * HD)
    n_slash, n_vert = slash.shape[1], vert.shape[1]
    width = (n_slash + n_vert) * BLK
    win_rows = sum(w.shape[0] for w in windows)
    dtype = qs[0].dtype
    pos = jnp.arange(BLK)
    causal = jnp.where(pos[:, None] > pos[None, :], MASKED, 0.0)
    masks = jnp.stack([jnp.zeros_like(causal), causal, jnp.full_like(causal, MASKED)]).astype(dtype)
    smem = pl.BlockSpec(memory_space=pltpu.SMEM)
    head_cols = pl.BlockSpec((dev_rows, group * HD), lambda e: (0, e))
    rows = heads * pair * local * group * BLK
    return pl.pallas_call(
        functools.partial(attend_kernel, (pair, local, group, reach, n_slash, n_vert)),
        grid=(heads,),
        in_specs=[smem] * 3
        + [head_cols] * pair
        + [pl.BlockSpec((w.shape[0], HD), lambda e: (0, e)) for w in windows]
        + [pl.BlockSpec((w.shape[0], HD), lambda e: (0, heads + e)) for w in windows]
        + [
            pl.BlockSpec((n_vert * BLK, 2 * HD), lambda e: (e, 0)),
            pl.BlockSpec((3, BLK, BLK), lambda e: (0, 0, 0)),
        ],
        out_specs=[head_cols] * pair,
        out_shape=[jax.ShapeDtypeStruct(q.shape, dtype) for q in qs],
        scratch_shapes=[
            pltpu.VMEM((win_rows, HD), dtype),
            pltpu.VMEM((win_rows, HD), dtype),
            pltpu.VMEM((width, 2 * HD), dtype),
            pltpu.VMEM((width, 2 * HD), dtype),
            pltpu.VMEM((group * BLK, 2 * HD), dtype),
            pltpu.VMEM((group * BLK, width), jnp.float32),
        ],
        compiler_params=pltpu.CompilerParams(vmem_limit_bytes=VMEM_LIMIT),
        cost_estimate=pl.CostEstimate(
            flops=8 * rows * width * HD,
            bytes_accessed=2 * (2 * win_rows * HD * heads + 2 * rows * HD),
            transcendentals=rows * width,
        ),
        name="attend",
    )(info, vert, slash, *qs, *windows, *windows, kv_vert, masks)


def body(queries, keys, values, vertical_blocks, slash_offsets, out_weight):
    tokens_dev = queries.shape[0]
    kv_heads = keys.shape[1] // HD
    local = tokens_dev // BLK
    size = lax.axis_size("ctx")
    pair = 2 if kv_heads % 2 == 0 and size % 2 == 0 else 1
    heads = kv_heads // pair
    chip_blocks = pair * local
    reach = -(-MAXOFF // chip_blocks)
    index = lax.axis_index("ctx")
    chip, core = index // pair, index % pair

    def mine(value, axis):
        span = value.shape[axis] // pair
        return lax.dynamic_slice_in_dim(value, core * span, span, axis)

    def theirs(value, axis):
        span = value.shape[axis] // pair
        return lax.dynamic_slice_in_dim(value, (1 - core) * span, span, axis)

    if pair == 2:
        kv_mine = jnp.concatenate([mine(keys, 1), mine(values, 1)], 1)
        kv_other = swapped(jnp.concatenate([theirs(keys, 1), theirs(values, 1)], 1))
        kv_chip = jnp.concatenate([kv_mine, kv_other], 0)
    else:
        kv_chip = jnp.concatenate([keys, values], 1)
    windows = [kv_chip] + [shifted(kv_chip, pair * d) for d in range(1, reach + 1)]
    if pair == 2:
        qs = [mine(queries, 1), swapped(theirs(queries, 1))]
    else:
        qs = [queries]
    vert, slash = mine(vertical_blocks, 0), mine(slash_offsets, 0)

    within = vert % chip_blocks
    if pair == 2:
        within = (within // local ^ core) * local + within % local
    owned = (vert // chip_blocks == chip).astype(jnp.int32)
    place = jnp.stack([within.reshape(-1), owned.reshape(-1)]).astype(jnp.int32)
    listed = pick_vertical(kv_chip, place, heads, vert.shape[1])
    groups = [list(range(c, size, pair)) for c in range(pair)]
    share = lax.psum_scatter(
        listed, "ctx", scatter_dimension=0, axis_index_groups=groups, tiled=True
    )
    kv_vert = lax.all_gather(share, "ctx", axis=0, axis_index_groups=groups, tiled=True)

    info = jnp.stack([chip, core]).astype(jnp.int32)
    att = attend(qs, windows, kv_vert, vert, slash, info, heads, local)
    if pair == 2:
        own, other = att[0], swapped(att[1])
        low, high = jnp.where(core == 0, own, other), jnp.where(core == 0, other, own)
        attended = jnp.concatenate([low, high], 1)
    else:
        attended = att[0]
    output = jnp.dot(
        lax.all_gather(attended, "head", axis=1, tiled=True),
        out_weight,
        preferred_element_type=jnp.float32,
    )
    return output.astype(jnp.bfloat16)


def solution(mesh):
    placed = (
        P("ctx", "head"),
        P("ctx", "head"),
        P("ctx", "head"),
        P("head", None),
        P("head", None),
        P(None, "head"),
    )
    return jax.shard_map(
        body, mesh=mesh, in_specs=placed, out_specs=P("ctx", "head"), check_vma=False
    )
```

time: 687 us -> 349 us (0.51)
  blocking collectives: 296 us -> 0 us
  waiting for transfers between devices: 0.01 us -> 175 us
  local copies, waits for them, and re-layouts: 141 us -> 8.15 us
  matrix products: 151 us -> 22.4 us
  Pallas kernels: 0 us -> 102 us
  other arithmetic: 75.9 us -> 5.57 us
  between operations: 0.12 us -> 13.5 us
  starting transfers between devices: 11.2 us -> 19.5 us
  loops' own time: 7.73 us -> 0 us
    psum x1 -> x0, blocking collectives: 296 us -> none  [body(): vertical_kv = lax.psum(masked, 'ctx').astype(jnp.bfloat16)]
    dot_general x9 -> x0, matrix products: 128 us -> none  [the longest x4 64.6 us: attend(): jnp.einsum('hgrjc,hjcd->rhgd', weights, keys_all[1], preferred_element_ty...]
    ppermute x4 -> x5, waiting for transfers between devices: 0.01 us -> 109 us  [the longest x2 104 us: shifted(): return lax.ppermute(value, 'ctx', pairs)]
    pallas_call x0 -> x2, Pallas kernels: none -> 102 us  [the longest x1 85.5 us: attend(): pl.pallas_call(functools.partial(attend_kernel, (pair, local, group, reac...]
    reduce_scatter x0 -> x1, waiting for transfers between devices: none -> 66.4 us  [body(): lax.psum_scatter(listed, 'ctx', scatter_dimension=0, axis_index_groups=gr...]
    reduce_sum x4 -> x0, other arithmetic: 57.3 us -> none  [attend(): total = jnp.sum(expo, axis=(3, 4), keepdims=True)]
    concatenate x1 -> x0, local copies, waits for them, and re-layouts: 48.2 us -> none  [body(): window = jnp.concatenate(pieces, 1).transpose(0, 3, 1, 2, 4)]
    gather x12 -> x0, local copies, waits for them, and re-layouts: 39.1 us -> none  [pick_blocks(): return jnp.take(heads, picks, axis=1)]
  transfers between devices with their start and end apart: 4 -> 7, of which waited for: 0 -> 5; matrix products, arithmetic and copies ran while one was open for 1% -> 2% of each run, Pallas kernels for 0% -> 0%
where the time goes in v1:
time: 349 us; the launch traced here: 347 us
  waiting for transfers between devices  175 us (50%)
  Pallas kernels  102 us (29%)
  matrix products  22.4 us (6%)
  starting transfers between devices  19.5 us (6%)
  between operations  13.5 us (4%)
  local copies, waits for them, and re-layouts  8.15 us (2%)
  other arithmetic  5.57 us (2%)
    ppermute x2, waiting for transfers between devices, shifted(): return lax.ppermute(value, 'ctx', pairs)  104 us
    pallas_call x1, Pallas kernels, attend(): pl.pallas_call(functools.partial(attend_kernel, (pair, local, group, reac...  85.5 us
    reduce_scatter x1, waiting for transfers between devices, body(): lax.psum_scatter(listed, 'ctx', scatter_dimension=0, axis_index_groups=gr...  66.4 us
    dot_general x1, matrix products, body(): jnp.dot(lax.all_gather(attended, 'head', axis=1, tiled=True), out_weight,...  22.4 us
    pallas_call x1, Pallas kernels, pick_vertical(): pl.pallas_call(pick_kernel, grid_spec=pltpu.PrefetchScalarGridSpec(num_sc...  16.5 us
    ppermute x3, starting transfers between devices, swapped(): return lax.ppermute(value, 'ctx', [(i, i ^ 1) for i in range(size)])  11.4 us
    ppermute x2, starting transfers between devices, shifted(): return lax.ppermute(value, 'ctx', pairs)  8.05 us
  transfers between devices with their start and end apart: 7, of which 5 were waited for; matrix products, arithmetic and copies ran while one was open for 2% of the time, Pallas kernels for 0%

profile of v1, /device:TPU:25, one launch (start us, length us, event | category | flops | bytes accessed | tf_op | source)
XLA Modules:
  0.0 346.5 jit_solution(1647427799441415024)
XLA Ops:
  6.5 1.7 constant_dynamic-slice_fusion.2
  8.2 0.1 pad_maximum_fusion.1
  8.4 0.7 collective-permute-start.1
  9.1 0.1 stack_reshape.9
  9.3 0.6 pad_add_fusion.place
  9.9 1.5 collective-permute-done.1
  11.4 1.5 pad_maximum_fusion.k_ref.v_ref.refs_2_.refs_5_
  12.9 16.5 %pick_vertical.1 = bf16[4096,256]{1,0:T(8,128)(2,1)} custom-call(s32[2,32]{1,0:T(2,128)} %pad_add_fusion.place, bf16[1024,1024]{1,0:T(8,128)(2,1)} %pad_maximum_fusion.k_ref.v_ref.refs_2_.refs_5_, bf16[1024,1024]{1,0:T(8,128)(2,1)} %pad_maximum_fusion.k_ref.v_ref.refs_2_.refs_5_), custom_call_target="tpu_custom_call" | custom-call | tf_op jit(solution)/shard_map/pick_vertical/pallas_call | solution.py:45
  29.5 66.4 %reduce-scatter.2.cloned.1.call-done = bf16[256,256]{1,0:T(8,128)(2,1)} async-done(((bf16[4096,256]{1,0:T(8,128)(2,1)}), bf16[256,256]{1,0:T(8,128)(2,1)}) %reduce-scatter.2.cloned.1.call-update) | async-done | bytes 131088 | tf_op jit(solution)/shard_map/reduce_scatter | solution.py:226
  95.9 4.2 %constant_dynamic-slice_fusion.4 = (bf16[512,2048]{1,0:T(8,128)(2,1)S(1)}, bf16[512,2048]{1,0:T(8,128)(2,1)}) fusion(bf16[512,4096]{1,0:T(8,128)(2,1)} %param.6, s32[]{:T(128)S(6)} %select_n.75, s32[]{:T(128)S(6)} %select_n.74), kind=kLoop, calls=%fused_computation.31 | loop fusion | bytes 8388616 | tf_op jit(solution)/shard_map/dynamic_slice | solution.py:204
  100.2 9.8 %collective-permute-start = (bf16[512,2048]{1,0:T(8,128)(2,1)S(1)}, bf16[512,2048]{1,0:T(8,128)(2,1)S(1)}, u32[]{:S(2)}, u32[]{:S(2)}) collective-permute-start(bf16[512,2048]{1,0:T(8,128)(2,1)S(1)} %get-tuple-element.13), channel_id=1, source_target_pairs={{0,1},{1,0},{2,3},{3,2},{4,5},{5,4},{6,7},{7,6},{8,9},{9,8},{10,11... | collective-permute-start | bytes 6291464 | tf_op jit(solution)/shard_map/ppermute | solution.py:26
  110.0 5.4 %collective-permute-start.3 = (bf16[1024,1024]{1,0:T(8,128)(2,1)S(1)}, bf16[1024,1024]{1,0:T(8,128)(2,1)S(1)}, u32[]{:S(2)}, u32[]{:S(2)}) collective-permute-start(bf16[1024,1024]{1,0:T(8,128)(2,1)S(1)} %copy-done.2), channel_id=1, source_target_pairs={{0,4},{1,5},{2,6},{3,7},{4,8},{5,9},{6,10},{7,11},{8,12},{9,13},{1... | collective-permute-start | bytes 6291464 | tf_op jit(solution)/shard_map/ppermute | solution.py:21
  115.4 2.7 collective-permute-start.2
  118.1 0.7 pad_add_fusion.1.info
  118.8 0.6 constant_dynamic-slice_fusion.6.slash
  119.4 0.7 maximum_maximum_fusion.refs_9_
  120.2 95.4 %collective-permute-done.3.refs_4_.refs_7_ = bf16[1024,1024]{1,0:T(8,128)(2,1)S(1)} collective-permute-done((bf16[1024,1024]{1,0:T(8,128)(2,1)S(1)}, bf16[1024,1024]{1,0:T(8,128)(2,1)S(1)}, u32[]{:S(2)}, u32[]{:S(2)}) %collective-permute-start.3) | collective-permute-done | bytes 2097184 | tf_op jit(solution)/shard_map/ppermute | solution.py:21
  215.5 1.4 copy-done.6
  216.9 8.1 %collective-permute-done.2.refs_3_.refs_6_ = bf16[1024,1024]{1,0:T(8,128)(2,1)} collective-permute-done((bf16[1024,1024]{1,0:T(8,128)(2,1)S(1)}, bf16[1024,1024]{1,0:T(8,128)(2,1)}, u32[]{:S(2)}, u32[]{:S(2)}) %collective-permute-start.2) | collective-permute-done | bytes 2097184 | tf_op jit(solution)/shard_map/ppermute | solution.py:21
  225.1 85.5 %attend.1 = (bf16[512,2048]{1,0:T(8,128)(2,1)}, bf16[512,2048]{1,0:T(8,128)(2,1)}) custom-call(s32[2]{0:T(128)} %pad_add_fusion.1.info, s32[4,8]{1,0:T(4,128)} %copy-done.3, s32[4,8]{1,0:T(4,128)} %constant_dynamic-slice_fusion.6.slash, bf16[512,2048]{1,0:T(8,128)(2,1)} %get-tuple-element.14.refs_0_, bf16[512,2048]{1,0:T(8,128)(2,1)} %copy-done.5, ...), custom_call_target="tpu_custom_call" | custom-call | flops 34359738368 | bytes 14680064 | tf_op jit(solution)/shard_map/attend/pallas_call | solution.py:155
  310.6 0.8 collective-permute-start.4
  311.4 4.0 %collective-permute-done.4 = bf16[512,2048]{1,0:T(8,128)(2,1)S(1)} collective-permute-done((bf16[512,2048]{1,0:T(8,128)(2,1)}, bf16[512,2048]{1,0:T(8,128)(2,1)S(1)}, u32[]{:S(2)}, u32[]{:S(2)}) %collective-permute-start.4) | collective-permute-done | bytes 2097184 | tf_op jit(solution)/shard_map/ppermute | solution.py:26
  315.4 1.9 broadcast_select_fusion.1
  317.3 22.4 %convolution_convert_fusion = bf16[512,4096]{1,0:T(8,128)(2,1)} fusion(bf16[4096,4096]{1,0:T(8,128)(2,1)} %param.11, bf16[512,2048]{1,0:T(8,128)(2,1)S(1)} %get-tuple-element.12, bf16[512,2048]{1,0:T(8,128)(2,1)S(1)} %get-tuple-element.11), kind=kOutput, calls=%fused_computation | convolution fusion | flops 17190354944 | bytes 41943040 | tf_op jit(solution)/shard_map/dot_general | solution.py:239
  (25 shorter events, 0.3 us)
Async XLA Ops:
  6.5 112.3 %copy-start = (s32[8,8]{1,0:T(8,128)S(1)}, s32[8,8]{1,0:T(8,128)}, u32[]{:S(2)}) copy-start(s32[8,8]{1,0:T(8,128)} %param.10) | copy-start | bytes 772
  6.5 89.4 %reduce-scatter.2.cloned.1.call-start = ((), (), s32[]{:S(2)}) async-start(), calls=%async_computation.1 | async-start | bytes 2228224 | tf_op jit(solution)/shard_map/reduce_scatter | solution.py:226
  8.2 0.9 copy-start.4
  8.4 3.0 collective-permute-start.1
  9.1 3.8 %copy-start.3 = (s32[4,8]{1,0:T(4,128)}, s32[4,8]{1,0:T(4,128)S(1)}, u32[]{:S(2)}) copy-start(s32[4,8]{1,0:T(4,128)S(1)} %get-tuple-element.10.vert) | copy-start | bytes 388
  29.5 195.6 %all-gather.2.cloned.1.call-start = ((), (), s32[]{:S(2)}) async-start(), calls=%async_computation.2 | async-start | bytes 2228224 | tf_op jit(solution)/shard_map/all_gather | solution.py:229
  95.9 14.0 %copy-start.2 = (bf16[1024,1024]{1,0:T(8,128)(2,1)S(1)}, bf16[1024,1024]{1,0:T(8,128)(2,1)}, u32[]{:S(2)}) copy-start(bf16[1024,1024]{1,0:T(8,128)(2,1)} %pad_maximum_fusion.k_ref.v_ref.refs_2_.refs_5_) | copy-start | bytes 6291460
  100.2 20.0 %collective-permute-start = (bf16[512,2048]{1,0:T(8,128)(2,1)S(1)}, bf16[512,2048]{1,0:T(8,128)(2,1)S(1)}, u32[]{:S(2)}, u32[]{:S(2)}) collective-permute-start(bf16[512,2048]{1,0:T(8,128)(2,1)S(1)} %get-tuple-element.13), channel_id=1, source_target_pairs={{0,1},{1,0},{2,3},{3,2},{4,5},{5,4},{6,7},{7,6},{8,9},{9,8},{10,11... | collective-permute-start | bytes 6291464 | tf_op jit(solution)/shard_map/ppermute | solution.py:26
  110.0 105.6 %collective-permute-start.3 = (bf16[1024,1024]{1,0:T(8,128)(2,1)S(1)}, bf16[1024,1024]{1,0:T(8,128)(2,1)S(1)}, u32[]{:S(2)}, u32[]{:S(2)}) collective-permute-start(bf16[1024,1024]{1,0:T(8,128)(2,1)S(1)} %copy-done.2), channel_id=1, source_target_pairs={{0,4},{1,5},{2,6},{3,7},{4,8},{5,9},{6,10},{7,11},{8,12},{9,13},{1... | collective-permute-start | bytes 6291464 | tf_op jit(solution)/shard_map/ppermute | solution.py:21
  115.4 109.7 %collective-permute-start.2 = (bf16[1024,1024]{1,0:T(8,128)(2,1)S(1)}, bf16[1024,1024]{1,0:T(8,128)(2,1)}, u32[]{:S(2)}, u32[]{:S(2)}) collective-permute-start(bf16[1024,1024]{1,0:T(8,128)(2,1)S(1)} %copy-done.2), channel_id=1, source_target_pairs={{0,2},{1,3},{2,4},{3,5},{4,6},{5,7},{6,8},{7,9},{8,10},{9,11},{10,... | collective-permute-start | bytes 6291464 | tf_op jit(solution)/shard_map/ppermute | solution.py:21
  120.1 104.9 %copy-start.5 = (bf16[512,2048]{1,0:T(8,128)(2,1)}, bf16[512,2048]{1,0:T(8,128)(2,1)S(1)}, u32[]{:S(2)}) copy-start(bf16[512,2048]{1,0:T(8,128)(2,1)S(1)} %collective-permute-done.refs_1_) | copy-start | bytes 6291460
  215.5 1.4 copy-start.6
  310.6 4.8 %collective-permute-start.4 = (bf16[512,2048]{1,0:T(8,128)(2,1)}, bf16[512,2048]{1,0:T(8,128)(2,1)S(1)}, u32[]{:S(2)}, u32[]{:S(2)}) collective-permute-start(bf16[512,2048]{1,0:T(8,128)(2,1)} %get-tuple-element.8), channel_id=1, source_target_pairs={{0,1},{1,0},{2,3},{3,2},{4,5},{5,4},{6,7},{7,6},{8,9},{9,8},{10,11... | collective-permute-start | bytes 6291464 | tf_op jit(solution)/shard_map/ppermute | solution.py:26
  317.3 22.4 %copy-start.1 = (s32[8,8]{1,0:T(8,128)S(1)}, s32[8,8]{1,0:T(8,128)}, u32[]{:S(2)}) copy-start(s32[8,8]{1,0:T(8,128)} %param.10) | copy-start | bytes 772
Sparse Core Ops, SparseCore 0:
  29.6 66.2 reduce-scatter.1
  98.7 122.4 all-gather.1

commit v2 on v1

v2 whole, which is shorter than its diff:
```python
import functools
import math

import jax
import jax.numpy as jnp
from jax import lax
from jax.experimental import pallas as pl
from jax.experimental.pallas import tpu as pltpu
from jax.sharding import PartitionSpec as P

HD = 128
BLK = 128
MAXOFF = 16
PLANE = 4
MASKED = -1e30
VMEM_LIMIT = 56 * 1024 * 1024


def shifted(value, by):
    size = lax.axis_size("ctx")
    return lax.ppermute(value, "ctx", [(i, i + by) for i in range(size - by)])


def crossed(value, bits):
    size = lax.axis_size("ctx")
    return lax.ppermute(value, "ctx", [(i, i ^ bits) for i in range(size)])


def prepare_kernel(cfg, info, vert, *refs):
    pair, local, heads, plane = cfg
    chip, core = info[0], info[1]
    keys, values = refs[:2]
    refs = refs[2:]
    other = None
    if pair > 1:
        other, refs = refs[0], refs[1:]
    chip_outs, refs = refs[:heads], refs[heads:]
    list_outs, chip_kv = refs[:plane], refs[plane]
    n_vert = vert.shape[1]
    dev_rows = local * BLK
    chip_blocks = pair * local
    for e in range(heads):
        at = pl.multiple_of((core * heads + e) * HD, HD)
        chip_kv[e, :dev_rows, :HD] = keys[:, pl.ds(at, HD)]
        chip_kv[e, :dev_rows, HD:] = values[:, pl.ds(at, HD)]
        if pair > 1:
            chip_kv[e, dev_rows:, :HD] = other[:, e * HD : (e + 1) * HD]
            chip_kv[e, dev_rows:, HD:] = other[:, (heads + e) * HD : (heads + e + 1) * HD]
        chip_outs[e][...] = chip_kv[e]
    per = heads * n_vert // plane
    for k in range(plane):
        for i in range(per):
            flat = (chip % plane ^ k) * per + i
            e, j = flat // n_vert, flat % n_vert
            block = vert[e, j]
            within = block % chip_blocks
            if pair > 1:
                within = (within // local ^ core) * local + within % local
            rows = slice(i * BLK, (i + 1) * BLK)
            owned = block // chip_blocks == chip
            found = chip_kv[e, pl.ds(pl.multiple_of(within * BLK, BLK), BLK), :]
            list_outs[k][rows, :] = jnp.where(owned, found, jnp.zeros_like(found))


def prepare(info, vert, keys, values, other, heads, local, plane):
    pair = 1 if other is None else 2
    chip_rows = pair * local * BLK
    per = heads * vert.shape[1] // plane
    dtype = keys.dtype
    smem = pl.BlockSpec(memory_space=pltpu.SMEM)
    vmem = pl.BlockSpec(memory_space=pltpu.VMEM)
    data = [keys, values] + ([] if other is None else [other])
    outs = pl.pallas_call(
        functools.partial(prepare_kernel, (pair, local, heads, plane)),
        in_specs=[smem] * 2 + [vmem] * len(data),
        out_specs=[vmem] * (heads + plane),
        out_shape=[jax.ShapeDtypeStruct((chip_rows, 2 * HD), dtype)] * heads
        + [jax.ShapeDtypeStruct((per * BLK, 2 * HD), dtype)] * plane,
        scratch_shapes=[pltpu.VMEM((heads, chip_rows, 2 * HD), dtype)],
        compiler_params=pltpu.CompilerParams(vmem_limit_bytes=VMEM_LIMIT),
        cost_estimate=pl.CostEstimate(
            flops=0, bytes_accessed=8 * heads * chip_rows * 2 * HD, transcendentals=0
        ),
        name="prepare",
    )(info, vert, *data)
    return outs[:heads], outs[heads:]


def attend_kernel(cfg, info, vert, slash, *refs):
    e, pair, local, group, reach, n_slash, n_vert, plane, heads = cfg
    q_refs, refs = refs[:pair], refs[pair:]
    w_refs, refs = refs[: reach + 1], refs[reach + 1 :]
    kv_vert, masks, refs = refs[0], refs[1], refs[2:]
    out_refs, refs = refs[:pair], refs[pair:]
    win, kg, vg, qx, sc = refs
    chip, core = info[0], info[1]
    dev_rows = local * BLK
    chip_blocks = pair * local
    chip_rows = chip_blocks * BLK
    width = (n_slash + n_vert) * BLK
    step = min(2 * BLK, width)
    factor = math.log2(math.e) / math.sqrt(HD)

    for back in range(reach + 1):
        for slot in range(pair):
            owner = core ^ slot if pair > 1 else 0
            at = pl.multiple_of((reach - back) * chip_rows + owner * dev_rows, dev_rows)
            win[pl.ds(at, dev_rows), :] = w_refs[back][slot * dev_rows : (slot + 1) * dev_rows, :]
    per = heads * n_vert // plane
    for j in range(n_vert):
        part, place = divmod(e * n_vert + j, per)
        src = pl.multiple_of(((part ^ chip % plane) * per + place) * BLK, BLK)
        rows = slice((n_slash + j) * BLK, (n_slash + j + 1) * BLK)
        kg[rows, :HD] = kv_vert[pl.ds(src, BLK), :HD]
        vg[rows, :HD] = kv_vert[pl.ds(src, BLK), HD:]
    vg[:, HD:] = jnp.ones((width, HD), vg.dtype)
    row = lax.broadcasted_iota(jnp.int32, (BLK, HD), 0)
    col = lax.broadcasted_iota(jnp.int32, (BLK, HD), 1)
    eye = jnp.where(row == col, 1.0, 0.0).astype(qx.dtype)
    for g in range(group):
        qx[g * BLK : (g + 1) * BLK, HD:] = eye

    for slot in range(pair):

        def one_block(b, carry, slot=slot):
            rel = (core ^ slot if pair > 1 else 0) * local + b
            here = chip * chip_blocks + rel
            starts = [here - slash[e, j] for j in range(n_slash)]
            for j in range(n_slash):
                off = slash[e, j]
                src = pl.multiple_of((reach * chip_blocks + rel - off) * BLK, BLK)
                rows = slice(j * BLK, (j + 1) * BLK)
                kg[rows, :HD] = win[pl.ds(src, BLK), :HD]
                vg[rows, :HD] = win[pl.ds(src, BLK), HD:]
                kind = jnp.where(starts[j] < 0, 2, jnp.where(off == 0, 1, 0))
                kg[rows, HD:] = masks[kind]
            for j in range(n_vert):
                block = vert[e, j]
                hidden = block >= here
                for start in starts:
                    hidden = hidden | (block == start)
                rows = slice((n_slash + j) * BLK, (n_slash + j + 1) * BLK)
                kg[rows, HD:] = masks[jnp.where(hidden, 2, 0)]
            q_rows = pl.ds(pl.multiple_of(b * BLK, BLK), BLK)
            for g in range(group):
                qx[g * BLK : (g + 1) * BLK, :HD] = q_refs[slot][q_rows, g * HD : (g + 1) * HD]
            top = None
            for t in range(0, width, step):
                s = lax.dot_general(
                    qx[...], kg[t : t + step, :], (((1,), (1,)), ((), ())),
                    preferred_element_type=jnp.float32,
                )
                sc[:, t : t + step] = s
                for u in range(0, step, HD):
                    piece = s[:, u : u + HD]
                    top = piece if top is None else jnp.maximum(top, piece)
            top = jnp.max(top, axis=1, keepdims=True)
            acc = None
            for t in range(0, width, step):
                p = jnp.exp2((sc[:, t : t + step] - top) * factor).astype(vg.dtype)
                o = jnp.dot(p, vg[t : t + step, :], preferred_element_type=jnp.float32)
                acc = o if acc is None else acc + o
            res = (acc[:, :HD] / acc[:, HD:]).astype(out_refs[slot].dtype)
            for g in range(group):
                out_refs[slot][q_rows, g * HD : (g + 1) * HD] = res[g * BLK : (g + 1) * BLK]
            return carry

        lax.fori_loop(0, local, one_block, 0)


def attend(e, queries, q_other, windows, kv_vert, masks, vert, slash, info, local, plane):
    pair, reach = (1 if q_other is None else 2), len(windows) - 1
    heads, (n_slash, n_vert) = vert.shape[0], (slash.shape[1], vert.shape[1])
    dev_rows = queries.shape[0]
    wide = queries.shape[1] // (pair * heads)
    group = wide // HD
    width = (n_slash + n_vert) * BLK
    win_rows = sum(w.shape[0] for w in windows)
    dtype = queries.dtype
    rows = pair * local * group * BLK
    q_specs = [pl.BlockSpec((dev_rows, wide), lambda i, info, *_: (0, info[1] * heads + e))]
    if pair > 1:
        q_specs.append(pl.BlockSpec((dev_rows, wide), lambda i, *_: (0, e)))

    def whole(a):
        return pl.BlockSpec(a.shape, lambda i, *_: (0,) * a.ndim)

    return pl.pallas_call(
        functools.partial(
            attend_kernel, (e, pair, local, group, reach, n_slash, n_vert, plane, heads)
        ),
        grid_spec=pltpu.PrefetchScalarGridSpec(
            num_scalar_prefetch=3,
            grid=(1,),
            in_specs=q_specs + [whole(w) for w in windows] + [whole(kv_vert), whole(masks)],
            out_specs=[pl.BlockSpec((dev_rows, wide), lambda i, *_: (0, 0))] * pair,
            scratch_shapes=[
                pltpu.VMEM((win_rows, 2 * HD), dtype),
                pltpu.VMEM((width, 2 * HD), dtype),
                pltpu.VMEM((width, 2 * HD), dtype),
                pltpu.VMEM((group * BLK, 2 * HD), dtype),
                pltpu.VMEM((group * BLK, width), jnp.float32),
            ],
        ),
        out_shape=[jax.ShapeDtypeStruct((dev_rows, wide), dtype)] * pair,
        compiler_params=pltpu.CompilerParams(vmem_limit_bytes=VMEM_LIMIT),
        cost_estimate=pl.CostEstimate(
            flops=8 * rows * width * HD,
            bytes_accessed=2 * (2 * win_rows * HD + 2 * rows * HD),
            transcendentals=rows * width,
        ),
        name="attend",
    )(info, vert, slash, *([queries] if pair == 1 else [queries, q_other]), *windows, kv_vert, masks)


def project_kernel(n, has_before, info, *refs):
    lefts, rights, refs = refs[:n], refs[n : 2 * n], refs[2 * n :]
    acc = refs[0][...] if has_before else None
    for left, right in zip(lefts, rights):
        part = jnp.dot(left[...], right[...], preferred_element_type=jnp.float32)
        acc = part if acc is None else acc + part
    refs[-1][...] = acc.astype(refs[-1].dtype)


def project(pieces, before, out_weight, info, heads, dtype):
    rows, wide = pieces[0][2].shape
    columns = out_weight.shape[1]
    tile = min(512, columns)
    n = len(pieces)

    def weight_spec(swap, e):
        if swap:
            return pl.BlockSpec((wide, tile), lambda i, info: ((1 - info[1]) * heads + e, i))
        return pl.BlockSpec((wide, tile), lambda i, info: (info[1] * heads + e, i))

    in_specs = [pl.BlockSpec((rows, wide), lambda i, info: (0, 0))] * n
    in_specs += [weight_spec(swap, e) for swap, e, _ in pieces]
    args = [a for _, _, a in pieces] + [out_weight] * n
    out_spec = pl.BlockSpec((rows, tile), lambda i, info: (0, i))
    if before is not None:
        in_specs.append(out_spec)
        args.append(before)
    return pl.pallas_call(
        functools.partial(project_kernel, n, before is not None),
        grid_spec=pltpu.PrefetchScalarGridSpec(
            num_scalar_prefetch=1, grid=(columns // tile,), in_specs=in_specs, out_specs=out_spec
        ),
        out_shape=jax.ShapeDtypeStruct((rows, columns), dtype),
        compiler_params=pltpu.CompilerParams(vmem_limit_bytes=VMEM_LIMIT),
        cost_estimate=pl.CostEstimate(
            flops=2 * n * rows * wide * columns,
            bytes_accessed=2 * n * wide * (rows + columns) + 8 * rows * columns,
            transcendentals=0,
        ),
        name="project",
    )(info, *args)


def body(queries, keys, values, vertical_blocks, slash_offsets, out_weight):
    tokens_dev = queries.shape[0]
    kv_heads = keys.shape[1] // HD
    local = tokens_dev // BLK
    size = lax.axis_size("ctx")
    pair = 2 if kv_heads % 2 == 0 and size % 2 == 0 and lax.axis_size("head") == 1 else 1
    chips = size // pair
    heads = kv_heads // pair
    plane = PLANE if chips % PLANE == 0 and heads * vertical_blocks.shape[1] % PLANE == 0 else 1
    chip_blocks = pair * local
    reach = -(-MAXOFF // chip_blocks)
    index = lax.axis_index("ctx")
    chip, core = index // pair, index % pair
    info = jnp.stack([chip, core]).astype(jnp.int32)
    pos = jnp.arange(BLK)
    causal = jnp.where(pos[:, None] > pos[None, :], MASKED, 0.0)
    masks = jnp.stack([jnp.zeros_like(causal), causal, jnp.full_like(causal, MASKED)])
    masks = masks.astype(queries.dtype)

    def part(value, axis, which):
        span = value.shape[axis] // pair
        return lax.dynamic_slice_in_dim(value, which * span, span, axis)

    vert, slash = part(vertical_blocks, 0, core), part(slash_offsets, 0, core)
    kv_other = q_other = None
    if pair == 2:
        away = 1 - core
        kv_other = crossed(jnp.concatenate([part(keys, 1, away), part(values, 1, away)], 1), 1)
        q_other = crossed(part(queries, 1, away), 1)
    own, listed = prepare(info, vert, keys, values, kv_other, heads, local, plane)

    total = listed[0]
    for k in range(1, plane):
        total = total + crossed(listed[k], k * pair)
    step = 1
    while step < chips // plane:
        total = total + shifted(total, step * plane * pair)
        step *= 2
    kv_vert = jnp.concatenate([total] + [crossed(total, k * pair) for k in range(1, plane)], 0)

    near, far = [], []
    for e in range(heads):
        windows = [own[e]]
        if pair == 2 and reach == 2 and chips % 2 == 0:
            two_back = shifted(own[e], 2 * pair)
            sent = jnp.where(chip % 2 == 0, own[e], two_back)
            windows += [crossed(sent, pair), two_back]
        else:
            windows += [shifted(own[e], pair * d) for d in range(1, reach + 1)]
        att = attend(e, queries, q_other, windows, kv_vert, masks, vert, slash, info, local, plane)
        near.append((False, e, att[0]))
        if pair == 2:
            far.append((True, e, crossed(att[1], 1)))
    if pair == 1:
        attended = jnp.concatenate([a for _, _, a in near], 1)
        attended = lax.all_gather(attended, "head", axis=1, tiled=True)
        output = jnp.dot(attended, out_weight, preferred_element_type=jnp.float32)
        return output.astype(jnp.bfloat16)
    first = None
    if heads > 1:
        first = project(near[:-1] + far[:-1], None, out_weight, info, heads, jnp.float32)
    return project(near[-1:] + far[-1:], first, out_weight, info, heads, jnp.bfloat16)


def solution(mesh):
    placed = (
        P("ctx", "head"),
        P("ctx", "head"),
        P("ctx", "head"),
        P("head", None),
        P("head", None),
        P(None, "head"),
    )
    return jax.shard_map(
        body, mesh=mesh, in_specs=placed, out_specs=P("ctx", "head"), check_vma=False
    )
```

time: 349 us -> 296 us (0.85)
  waiting for transfers between devices: 175 us -> 83.5 us
  starting transfers between devices: 19.5 us -> 58.3 us
  Pallas kernels: 102 us -> 136 us
  matrix products: 22.4 us -> 0 us
  between operations: 13.5 us -> 0.2 us
    reduce_scatter x1 -> x0, waiting for transfers between devices: 66.4 us -> none  [body(): lax.psum_scatter(listed, 'ctx', scatter_dimension=0, axis_index_groups=gr...]
    ppermute x5 -> x22, starting transfers between devices: 19.4 us -> 58.3 us  [the longest x16 47.7 us: crossed(): return lax.ppermute(value, 'ctx', [(i, i ^ bits) for i in range(size)])]
    pallas_call x2 -> x7, Pallas kernels: 102 us -> 136 us  [the longest x4 97.5 us: attend(): pl.pallas_call(functools.partial(attend_kernel, (e, pair, local, group, r...]
    ppermute x5 -> x22, waiting for transfers between devices: 109 us -> 83.5 us  [the longest x16 47.6 us: crossed(): return lax.ppermute(value, 'ctx', [(i, i ^ bits) for i in range(size)])]
    dot_general x1 -> x0, matrix products: 22.4 us -> none  [body(): jnp.dot(lax.all_gather(attended, 'head', axis=1, tiled=True), out_weight,...]
    unnamed x14 -> x36, local copies, waits for them, and re-layouts: 1.41 us -> 6.14 us
  transfers between devices with their start and end apart: 7 -> 22, of which waited for: 5 -> 11; matrix products, arithmetic and copies ran while one was open for 2% -> 3% of each run, Pallas kernels for 0% -> 40%
where the time goes in v2:
time: 296 us; the launch traced here: 295 us
  Pallas kernels  136 us (46%)
  waiting for transfers between devices  83.5 us (28%)
  starting transfers between devices  58.3 us (20%)
  local copies, waits for them, and re-layouts  10.4 us (4%)
  other arithmetic  7.01 us (2%)
    pallas_call x4, Pallas kernels, attend(): pl.pallas_call(functools.partial(attend_kernel, (e, pair, local, group, r...  97.5 us
    ppermute x16, starting transfers between devices, crossed(): return lax.ppermute(value, 'ctx', [(i, i ^ bits) for i in range(size)])  47.7 us
    ppermute x16, waiting for transfers between devices, crossed(): return lax.ppermute(value, 'ctx', [(i, i ^ bits) for i in range(size)])  47.6 us
    ppermute x6, waiting for transfers between devices, shifted(): return lax.ppermute(value, 'ctx', [(i, i + by) for i in range(size - by)])  35.9 us
    pallas_call x2, Pallas kernels, project(): pl.pallas_call(functools.partial(project_kernel, n, before is not None),...  33.8 us
    ppermute x6, starting transfers between devices, shifted(): return lax.ppermute(value, 'ctx', [(i, i + by) for i in range(size - by)])  10.6 us
    unnamed x36, local copies, waits for them, and re-layouts  6.14 us
  transfers between devices with their start and end apart: 22, of which 11 were waited for; matrix products, arithmetic and copies ran while one was open for 3% of the time, Pallas kernels for 40%

profile of v2, /device:TPU:25, one launch (start us, length us, event | category | flops | bytes accessed | tf_op | source)
XLA Modules:
  0.0 295.2 jit_solution(12678932697144336516)
XLA Ops:
  5.4 4.5 %prepare.1 = (bf16[1024,256]{1,0:T(8,128)(2,1)}, bf16[1024,256]{1,0:T(8,128)(2,1)}, bf16[1024,256]{1,0:T(8,128)(2,1)}, bf16[1024,256]{1,0:T(8,128)(2,1)}, bf16[1...) custom-call(s32[2]{0:T(128)} %pad_add_fusion.info, ...), custom_call_target="tpu_custom_call" | custom-call | bytes 8388608 | tf_op jit(solution)/shard_map/prepare/pallas_call | solution.py:73
  12.6 1.7 constant_dynamic-slice_fusion.2
  15.7 7.6 %collective-permute-done.4 = bf16[1024,256]{1,0:T(8,128)(2,1)S(1)} collective-permute-done((bf16[1024,256]{1,0:T(8,128)(2,1)}, bf16[1024,256]{1,0:T(8,128)(2,1)S(1)}, u32[]{:S(2)}, u32[]{:S(2)}) %collective-permute-start.4) | collective-permute-done | bytes 524320 | tf_op jit(solution)/shard_map/ppermute | solution.py:26
  24.2 11.3 %collective-permute-done.6 = bf16[1024,256]{1,0:T(8,128)(2,1)} collective-permute-done((bf16[1024,256]{1,0:T(8,128)(2,1)}, bf16[1024,256]{1,0:T(8,128)(2,1)}, u32[]{:S(2)}, u32[]{:S(2)}) %collective-permute-start.6) | collective-permute-done | bytes 524320 | tf_op jit(solution)/shard_map/ppermute | solution.py:26
  35.5 1.5 add_add_fusion
  38.4 2.1 collective-permute-start.2
  40.5 1.9 collective-permute-start.13
  43.9 1.9 collective-permute-start.15
  45.8 5.1 %collective-permute-done.7 = bf16[1024,256]{1,0:T(8,128)(2,1)S(1)} collective-permute-done((bf16[1024,256]{1,0:T(8,128)(2,1)S(1)}, bf16[1024,256]{1,0:T(8,128)(2,1)S(1)}, u32[]{:S(2)}, u32[]{:S(2)}) %collective-permute-start.7) | collective-permute-done | bytes 524320 | tf_op jit(solution)/shard_map/ppermute | solution.py:21
  50.8 1.9 collective-permute-start.17
  52.9 8.2 %collective-permute-done.2.refs_4_ = bf16[1024,256]{1,0:T(8,128)(2,1)} collective-permute-done((bf16[1024,256]{1,0:T(8,128)(2,1)}, bf16[1024,256]{1,0:T(8,128)(2,1)}, u32[]{:S(2)}, u32[]{:S(2)}) %collective-permute-start.2) | collective-permute-done | bytes 524320 | tf_op jit(solution)/shard_map/ppermute | solution.py:21
  63.7 8.7 %collective-permute-done.13.refs_4_ = bf16[1024,256]{1,0:T(8,128)(2,1)} collective-permute-done((bf16[1024,256]{1,0:T(8,128)(2,1)}, bf16[1024,256]{1,0:T(8,128)(2,1)}, u32[]{:S(2)}, u32[]{:S(2)}) %collective-permute-start.13) | collective-permute-done | bytes 524320 | tf_op jit(solution)/shard_map/ppermute | solution.py:21
  73.5 14.0 %collective-permute-done.8 = bf16[1024,256]{1,0:T(8,128)(2,1)S(1)} collective-permute-done((bf16[1024,256]{1,0:T(8,128)(2,1)S(1)}, bf16[1024,256]{1,0:T(8,128)(2,1)S(1)}, u32[]{:S(2)}, u32[]{:S(2)}) %collective-permute-start.8) | collective-permute-done | bytes 524320 | tf_op jit(solution)/shard_map/ppermute | solution.py:21
  87.6 31.9 %collective-permute-start.11 = (bf16[1024,256]{1,0:T(8,128)(2,1)S(1)}, bf16[1024,256]{1,0:T(8,128)(2,1)S(1)}, u32[]{:S(2)}, u32[]{:S(2)}) collective-permute-start(bf16[1024,256]{1,0:T(8,128)(2,1)S(1)} %add.46), channel_id=1, source_target_pairs={{0,6},{1,7},{2,4},{3,5},{4,2},{5,3},{6,0},{7,1},{8,14},{9,15},{10,... | collective-permute-start | bytes 1572872 | tf_op jit(solution)/shard_map/ppermute | solution.py:26
  121.2 8.0 %collective-permute-done.11 = bf16[1024,256]{1,0:T(8,128)(2,1)S(1)} collective-permute-done((bf16[1024,256]{1,0:T(8,128)(2,1)S(1)}, bf16[1024,256]{1,0:T(8,128)(2,1)S(1)}, u32[]{:S(2)}, u32[]{:S(2)}) %collective-permute-start.11) | collective-permute-done | bytes 524320 | tf_op jit(solution)/shard_map/ppermute | solution.py:26
  129.2 13.8 %collective-permute-done.10 = bf16[1024,256]{1,0:T(8,128)(2,1)S(1)} collective-permute-done((bf16[1024,256]{1,0:T(8,128)(2,1)S(1)}, bf16[1024,256]{1,0:T(8,128)(2,1)S(1)}, u32[]{:S(2)}, u32[]{:S(2)}) %collective-permute-start.10) | collective-permute-done | bytes 524320 | tf_op jit(solution)/shard_map/ppermute | solution.py:26
  146.0 4.7 %collective-permute-done.14.refs_3_ = bf16[1024,256]{1,0:T(8,128)(2,1)S(1)} collective-permute-done((bf16[1024,256]{1,0:T(8,128)(2,1)S(1)}, bf16[1024,256]{1,0:T(8,128)(2,1)S(1)}, u32[]{:S(2)}, u32[]{:S(2)}) %collective-permute-start.14) | collective-permute-done | bytes 524320 | tf_op jit(solution)/shard_map/ppermute | solution.py:26
  151.5 24.3 %attend.5 = (bf16[512,512]{1,0:T(8,128)(2,1)}, bf16[512,512]{1,0:T(8,128)(2,1)}) custom-call(s32[2]{0:T(128)} %pad_add_fusion.info, s32[4,8]{1,0:T(4,128)} %constant_dynamic-slice_fusion.4.vert, s32[4,8]{1,0:T(4,128)} %constant_dynamic-slice_fusion.3.slash, bf16[512,4096]{1,0:T(8,128)(2,1)} %refs_0_.9, bf16[512,2048]{1,0:T(8,128)(2,1)} %collective-permute-done.refs_1_, ...), custom_call_target="tpu_custom_call" | custom-call | flops 8589934592 | bytes 3670016 | tf_op jit(solution)/shard_map/attend/pallas_call | solution.py:188
  175.9 7.4 %collective-permute-start.19 = (bf16[512,512]{1,0:T(8,128)(2,1)}, bf16[512,512]{1,0:T(8,128)(2,1)S(1)}, u32[]{:S(2)}, u32[]{:S(2)}) collective-permute-start(bf16[512,512]{1,0:T(8,128)(2,1)} %get-tuple-element.34), channel_id=1, source_target_pairs={{0,1},{1,0},{2,3},{3,2},{4,5},{5,4},{6,7},{7,6},{8,9},{9,8},{10,11... | collective-permute-start | bytes 1572872 | tf_op jit(solution)/shard_map/ppermute | solution.py:26
  184.1 24.4 %attend.6 = (bf16[512,512]{1,0:T(8,128)(2,1)}, bf16[512,512]{1,0:T(8,128)(2,1)}) custom-call(s32[2]{0:T(128)} %pad_add_fusion.info, s32[4,8]{1,0:T(4,128)} %constant_dynamic-slice_fusion.4.vert, s32[4,8]{1,0:T(4,128)} %constant_dynamic-slice_fusion.3.slash, bf16[512,4096]{1,0:T(8,128)(2,1)} %refs_0_.9, bf16[512,2048]{1,0:T(8,128)(2,1)} %collective-permute-done.refs_1_, ...), custom_call_target="tpu_custom_call" | custom-call | flops 8589934592 | bytes 3670016 | tf_op jit(solution)/shard_map/attend/pallas_call | solution.py:188
  209.2 24.5 %attend.7 = (bf16[512,512]{1,0:T(8,128)(2,1)}, bf16[512,512]{1,0:T(8,128)(2,1)}) custom-call(s32[2]{0:T(128)} %pad_add_fusion.info, s32[4,8]{1,0:T(4,128)} %constant_dynamic-slice_fusion.4.vert, s32[4,8]{1,0:T(4,128)} %constant_dynamic-slice_fusion.3.slash, bf16[512,4096]{1,0:T(8,128)(2,1)} %refs_0_.9, bf16[512,2048]{1,0:T(8,128)(2,1)} %collective-permute-done.refs_1_, ...), custom_call_target="tpu_custom_call" | custom-call | flops 8589934592 | bytes 3670016 | tf_op jit(solution)/shard_map/attend/pallas_call | solution.py:188
  235.1 24.3 %attend.4 = (bf16[512,512]{1,0:T(8,128)(2,1)}, bf16[512,512]{1,0:T(8,128)(2,1)}) custom-call(s32[2]{0:T(128)} %pad_add_fusion.info, s32[4,8]{1,0:T(4,128)} %constant_dynamic-slice_fusion.4.vert, s32[4,8]{1,0:T(4,128)} %constant_dynamic-slice_fusion.3.slash, bf16[512,4096]{1,0:T(8,128)(2,1)} %refs_0_.9, bf16[512,2048]{1,0:T(8,128)(2,1)} %collective-permute-done.refs_1_, ...), custom_call_target="tpu_custom_call" | custom-call | flops 8589934592 | bytes 3670016 | tf_op jit(solution)/shard_map/attend/pallas_call | solution.py:188
  260.6 20.8 %project.2.refs_4_ = f32[512,4096]{1,0:T(8,128)} custom-call(s32[2]{0:T(128)} %pad_add_fusion.info, bf16[512,512]{1,0:T(8,128)(2,1)} %get-tuple-element.29.refs_0_, bf16[512,512]{1,0:T(8,128)(2,1)} %get-tuple-element.31.refs_1_, bf16[512,512]{1,0:T(8,128)(2,1)} %get-tuple-element.33.refs_2_, bf16[512,512]{1,0:T(8,128)(2,1)} %copy-done.3, ...), custom_call_target="tpu_custom_call" | custom-call | flops 12884901888 | bytes 45088768 | tf_op jit(solution)/shard_map/project/pallas_call | solution.py:243
  282.2 13.0 %project.3 = bf16[512,4096]{1,0:T(8,128)(2,1)} custom-call(s32[2]{0:T(128)} %pad_add_fusion.info, bf16[512,512]{1,0:T(8,128)(2,1)} %get-tuple-element.26.refs_0_, bf16[512,512]{1,0:T(8,128)(2,1)} %copy-done.6, bf16[4096,4096]{1,0:T(8,128)(2,1)} %refs_3_.1, bf16[4096,4096]{1,0:T(8,128)(2,1)} %refs_3_.1, f32[512,4096]{1,0:T(8,128)} %project.2.refs_4_), custom_call_target="tpu_custom_call" | custom-call | flops 4294967296 | bytes 26214400 | tf_op jit(solution)/shard_map/project/pallas_call | solution.py:243
  (81 shorter events, 27.4 us)
Async XLA Ops:
  1.4 3.0 %collective-permute-start.1 = (bf16[512,1024]{1,0:T(8,128)(2,1)S(1)}, bf16[512,1024]{1,0:T(8,128)(2,1)S(1)}, u32[]{:S(2)}, u32[]{:S(2)}) collective-permute-start(bf16[512,1024]{1,0:T(8,128)(2,1)S(1)} %pad_maximum_fusion.1), channel_id=1, source_target_pairs={{0,1},{1,0},{2,3},{3,2},{4,5},{5,4},{6,7},{7,6},{8,9},{9,8},{10,11... | collective-permute-start | bytes 3145736 | tf_op jit(solution)/shard_map/ppermute | solution.py:26
  9.9 13.4 %collective-permute-start.4 = (bf16[1024,256]{1,0:T(8,128)(2,1)}, bf16[1024,256]{1,0:T(8,128)(2,1)S(1)}, u32[]{:S(2)}, u32[]{:S(2)}) collective-permute-start(bf16[1024,256]{1,0:T(8,128)(2,1)} %get-tuple-element.23), channel_id=1, source_target_pairs={{0,2},{1,3},{2,0},{3,1},{4,6},{5,7},{6,4},{7,5},{8,10},{9,11},{10,... | collective-permute-start | bytes 1572872 | tf_op jit(solution)/shard_map/ppermute | solution.py:26
  11.2 13.0 %collective-permute-start.5 = (bf16[1024,256]{1,0:T(8,128)(2,1)}, bf16[1024,256]{1,0:T(8,128)(2,1)}, u32[]{:S(2)}, u32[]{:S(2)}) collective-permute-start(bf16[1024,256]{1,0:T(8,128)(2,1)} %get-tuple-element.24), channel_id=1, source_target_pairs={{0,4},{1,5},{2,6},{3,7},{4,0},{5,1},{6,2},{7,3},{8,12},{9,13},{10,... | collective-permute-start | bytes 1572872 | tf_op jit(solution)/shard_map/ppermute | solution.py:26
  12.4 23.1 %collective-permute-start.6 = (bf16[1024,256]{1,0:T(8,128)(2,1)}, bf16[1024,256]{1,0:T(8,128)(2,1)}, u32[]{:S(2)}, u32[]{:S(2)}) collective-permute-start(bf16[1024,256]{1,0:T(8,128)(2,1)} %get-tuple-element.25), channel_id=1, source_target_pairs={{0,6},{1,7},{2,4},{3,5},{4,2},{5,3},{6,0},{7,1},{8,14},{9,15},{10,... | collective-permute-start | bytes 1572872 | tf_op jit(solution)/shard_map/ppermute | solution.py:26
  14.3 131.7 %collective-permute-start = (bf16[512,2048]{1,0:T(8,128)(2,1)S(1)}, bf16[512,2048]{1,0:T(8,128)(2,1)}, u32[]{:S(2)}, u32[]{:S(2)}) collective-permute-start(bf16[512,2048]{1,0:T(8,128)(2,1)S(1)} %constant_dynamic-slice_fusion.2), channel_id=1, source_target_pairs={{0,1},{1,0},{2,3},{3,2},{4,5},{5,4},{6,7},{7,6},{8,9},{9,8},{10,11... | collective-permute-start | bytes 6291464 | tf_op jit(solution)/shard_map/ppermute | solution.py:26
  37.1 13.8 %collective-permute-start.7 = (bf16[1024,256]{1,0:T(8,128)(2,1)S(1)}, bf16[1024,256]{1,0:T(8,128)(2,1)S(1)}, u32[]{:S(2)}, u32[]{:S(2)}) collective-permute-start(bf16[1024,256]{1,0:T(8,128)(2,1)S(1)} %add_add_fusion), channel_id=1, source_target_pairs={{0,8},{1,9},{2,10},{3,11},{4,12},{5,13},{6,14},{7,15},{8,16},{9,17... | collective-permute-start | bytes 1572872 | tf_op jit(solution)/shard_map/ppermute | solution.py:21
  38.4 22.8 %collective-permute-start.2 = (bf16[1024,256]{1,0:T(8,128)(2,1)}, bf16[1024,256]{1,0:T(8,128)(2,1)}, u32[]{:S(2)}, u32[]{:S(2)}) collective-permute-start(bf16[1024,256]{1,0:T(8,128)(2,1)} %get-tuple-element.21.refs_2_), channel_id=1, source_target_pairs={{0,4},{1,5},{2,6},{3,7},{4,8},{5,9},{6,10},{7,11},{8,12},{9,13},{1... | collective-permute-start | bytes 1572872 | tf_op jit(solution)/shard_map/ppermute | solution.py:21
  40.5 31.8 %collective-permute-start.13 = (bf16[1024,256]{1,0:T(8,128)(2,1)}, bf16[1024,256]{1,0:T(8,128)(2,1)}, u32[]{:S(2)}, u32[]{:S(2)}) collective-permute-start(bf16[1024,256]{1,0:T(8,128)(2,1)} %get-tuple-element.28.refs_2_), channel_id=1, source_target_pairs={{0,4},{1,5},{2,6},{3,7},{4,8},{5,9},{6,10},{7,11},{8,12},{9,13},{1... | collective-permute-start | bytes 1572872 | tf_op jit(solution)/shard_map/ppermute | solution.py:21
  43.1 76.8 %copy-start.10 = (bf16[1024,256]{1,0:T(8,128)(2,1)S(1)}, bf16[1024,256]{1,0:T(8,128)(2,1)}, u32[]{:S(2)}) copy-start(bf16[1024,256]{1,0:T(8,128)(2,1)} %get-tuple-element.30.refs_2_) | copy-start | bytes 1572868
  43.1 78.1 %copy-start.9 = (bf16[1024,256]{1,0:T(8,128)(2,1)S(1)}, bf16[1024,256]{1,0:T(8,128)(2,1)}, u32[]{:S(2)}) copy-start(bf16[1024,256]{1,0:T(8,128)(2,1)} %get-tuple-element.32.refs_2_) | copy-start | bytes 1572868
  43.9 75.6 %collective-permute-start.15 = (bf16[1024,256]{1,0:T(8,128)(2,1)}, bf16[1024,256]{1,0:T(8,128)(2,1)S(1)}, u32[]{:S(2)}, u32[]{:S(2)}) collective-permute-start(bf16[1024,256]{1,0:T(8,128)(2,1)} %get-tuple-element.30.refs_2_), channel_id=1, source_target_pairs={{0,4},{1,5},{2,6},{3,7},{4,8},{5,9},{6,10},{7,11},{8,12},{9,13},{1... | collective-permute-start | bytes 1572872 | tf_op jit(solution)/shard_map/ppermute | solution.py:21
  50.8 69.1 %collective-permute-start.17 = (bf16[1024,256]{1,0:T(8,128)(2,1)}, bf16[1024,256]{1,0:T(8,128)(2,1)S(1)}, u32[]{:S(2)}, u32[]{:S(2)}) collective-permute-start(bf16[1024,256]{1,0:T(8,128)(2,1)} %get-tuple-element.32.refs_2_), channel_id=1, source_target_pairs={{0,4},{1,5},{2,6},{3,7},{4,8},{5,9},{6,10},{7,11},{8,12},{9,13},{1... | collective-permute-start | bytes 1572872 | tf_op jit(solution)/shard_map/ppermute | solution.py:21
  61.1 26.3 %collective-permute-start.8 = (bf16[1024,256]{1,0:T(8,128)(2,1)S(1)}, bf16[1024,256]{1,0:T(8,128)(2,1)S(1)}, u32[]{:S(2)}, u32[]{:S(2)}) collective-permute-start(bf16[1024,256]{1,0:T(8,128)(2,1)S(1)} %add.45), channel_id=1, source_target_pairs={{0,16},{1,17},{2,18},{3,19},{4,20},{5,21},{6,22},{7,23},{8,24},{9,... | collective-permute-start | bytes 1572872 | tf_op jit(solution)/shard_map/ppermute | solution.py:21
  87.6 41.7 %collective-permute-start.11 = (bf16[1024,256]{1,0:T(8,128)(2,1)S(1)}, bf16[1024,256]{1,0:T(8,128)(2,1)S(1)}, u32[]{:S(2)}, u32[]{:S(2)}) collective-permute-start(bf16[1024,256]{1,0:T(8,128)(2,1)S(1)} %add.46), channel_id=1, source_target_pairs={{0,6},{1,7},{2,4},{3,5},{4,2},{5,3},{6,0},{7,1},{8,14},{9,15},{10,... | collective-permute-start | bytes 1572872 | tf_op jit(solution)/shard_map/ppermute | solution.py:26
  119.5 23.6 %collective-permute-start.10 = (bf16[1024,256]{1,0:T(8,128)(2,1)S(1)}, bf16[1024,256]{1,0:T(8,128)(2,1)S(1)}, u32[]{:S(2)}, u32[]{:S(2)}) collective-permute-start(bf16[1024,256]{1,0:T(8,128)(2,1)S(1)} %add.46), channel_id=1, source_target_pairs={{0,4},{1,5},{2,6},{3,7},{4,0},{5,1},{6,2},{7,3},{8,12},{9,13},{10,... | collective-permute-start | bytes 1572872 | tf_op jit(solution)/shard_map/ppermute | solution.py:26
  119.5 23.6 %collective-permute-start.9 = (bf16[1024,256]{1,0:T(8,128)(2,1)S(1)}, bf16[1024,256]{1,0:T(8,128)(2,1)S(1)}, u32[]{:S(2)}, u32[]{:S(2)}) collective-permute-start(bf16[1024,256]{1,0:T(8,128)(2,1)S(1)} %add.46), channel_id=1, source_target_pairs={{0,2},{1,3},{2,0},{3,1},{4,6},{5,7},{6,4},{7,5},{8,10},{9,11},{10,... | collective-permute-start | bytes 1572872 | tf_op jit(solution)/shard_map/ppermute | solution.py:26
  119.9 30.8 %collective-permute-start.14 = (bf16[1024,256]{1,0:T(8,128)(2,1)S(1)}, bf16[1024,256]{1,0:T(8,128)(2,1)S(1)}, u32[]{:S(2)}, u32[]{:S(2)}) collective-permute-start(bf16[1024,256]{1,0:T(8,128)(2,1)S(1)} %broadcast_select_fusion.2), channel_id=1, source_target_pairs={{0,2},{1,3},{2,0},{3,1},{4,6},{5,7},{6,4},{7,5},{8,10},{9,11},{10,... | collective-permute-start | bytes 1572872 | tf_op jit(solution)/shard_map/ppermute | solution.py:26
  129.2 105.0 %collective-permute-start.3 = (bf16[1024,256]{1,0:T(8,128)(2,1)S(1)}, bf16[1024,256]{1,0:T(8,128)(2,1)S(1)}, u32[]{:S(2)}, u32[]{:S(2)}) collective-permute-start(bf16[1024,256]{1,0:T(8,128)(2,1)S(1)} %broadcast_select_fusion.3), channel_id=1, source_target_pairs={{0,2},{1,3},{2,0},{3,1},{4,6},{5,7},{6,4},{7,5},{8,10},{9,11},{10,... | collective-permute-start | bytes 1572872 | tf_op jit(solution)/shard_map/ppermute | solution.py:26
  143.1 40.2 %collective-permute-start.16 = (bf16[1024,256]{1,0:T(8,128)(2,1)S(1)}, bf16[1024,256]{1,0:T(8,128)(2,1)S(1)}, u32[]{:S(2)}, u32[]{:S(2)}) collective-permute-start(bf16[1024,256]{1,0:T(8,128)(2,1)S(1)} %broadcast_select_fusion.1), channel_id=1, source_target_pairs={{0,2},{1,3},{2,0},{3,1},{4,6},{5,7},{6,4},{7,5},{8,10},{9,11},{10,... | collective-permute-start | bytes 1572872 | tf_op jit(solution)/shard_map/ppermute | solution.py:26
  143.1 65.4 %collective-permute-start.18 = (bf16[1024,256]{1,0:T(8,128)(2,1)S(1)}, bf16[1024,256]{1,0:T(8,128)(2,1)S(1)}, u32[]{:S(2)}, u32[]{:S(2)}) collective-permute-start(bf16[1024,256]{1,0:T(8,128)(2,1)S(1)} %broadcast_select_fusion), channel_id=1, source_target_pairs={{0,2},{1,3},{2,0},{3,1},{4,6},{5,7},{6,4},{7,5},{8,10},{9,11},{10,... | collective-permute-start | bytes 1572872 | tf_op jit(solution)/shard_map/ppermute | solution.py:26
  175.9 83.6 %collective-permute-start.19 = (bf16[512,512]{1,0:T(8,128)(2,1)}, bf16[512,512]{1,0:T(8,128)(2,1)S(1)}, u32[]{:S(2)}, u32[]{:S(2)}) collective-permute-start(bf16[512,512]{1,0:T(8,128)(2,1)} %get-tuple-element.34), channel_id=1, source_target_pairs={{0,1},{1,0},{2,3},{3,2},{4,5},{5,4},{6,7},{7,6},{8,9},{9,8},{10,11... | collective-permute-start | bytes 1572872 | tf_op jit(solution)/shard_map/ppermute | solution.py:26
  208.4 51.0 %collective-permute-start.20 = (bf16[512,512]{1,0:T(8,128)(2,1)}, bf16[512,512]{1,0:T(8,128)(2,1)S(1)}, u32[]{:S(2)}, u32[]{:S(2)}) collective-permute-start(bf16[512,512]{1,0:T(8,128)(2,1)} %get-tuple-element.35), channel_id=1, source_target_pairs={{0,1},{1,0},{2,3},{3,2},{4,5},{5,4},{6,7},{7,6},{8,9},{9,8},{10,11... | collective-permute-start | bytes 1572872 | tf_op jit(solution)/shard_map/ppermute | solution.py:26
  233.8 25.7 %collective-permute-start.21 = (bf16[512,512]{1,0:T(8,128)(2,1)}, bf16[512,512]{1,0:T(8,128)(2,1)S(1)}, u32[]{:S(2)}, u32[]{:S(2)}) collective-permute-start(bf16[512,512]{1,0:T(8,128)(2,1)} %get-tuple-element.36), channel_id=1, source_target_pairs={{0,1},{1,0},{2,3},{3,2},{4,5},{5,4},{6,7},{7,6},{8,9},{9,8},{10,11... | collective-permute-start | bytes 1572872 | tf_op jit(solution)/shard_map/ppermute | solution.py:26
  259.4 22.0 %collective-permute-start.12 = (bf16[512,512]{1,0:T(8,128)(2,1)}, bf16[512,512]{1,0:T(8,128)(2,1)S(1)}, u32[]{:S(2)}, u32[]{:S(2)}) collective-permute-start(bf16[512,512]{1,0:T(8,128)(2,1)} %get-tuple-element.27), channel_id=1, source_target_pairs={{0,1},{1,0},{2,3},{3,2},{4,5},{5,4},{6,7},{7,6},{8,9},{9,8},{10,11... | collective-permute-start | bytes 1572872 | tf_op jit(solution)/shard_map/ppermute | solution.py:26
  (16 other events, 206.5 us)

commit v3 on v2

--- a/solution.py
+++ b/solution.py
@@ -92,7 +92,8 @@
     w_refs, refs = refs[: reach + 1], refs[reach + 1 :]
     kv_vert, masks, refs = refs[0], refs[1], refs[2:]
     out_refs, refs = refs[:pair], refs[pair:]
-    win, kg, vg, qx, sc = refs
+    win, kg, qx, res = refs[:4]
+    vgs, scs, tops, ps = refs[4:6], refs[6:8], refs[8:10], refs[10:12]
     chip, core = info[0], info[1]
     dev_rows = local * BLK
     chip_blocks = pair * local
@@ -107,65 +108,110 @@
             at = pl.multiple_of((reach - back) * chip_rows + owner * dev_rows, dev_rows)
             win[pl.ds(at, dev_rows), :] = w_refs[back][slot * dev_rows : (slot + 1) * dev_rows, :]
     per = heads * n_vert // plane
+    ones = jnp.ones((width, HD), vgs[0].dtype)
     for j in range(n_vert):
         part, place = divmod(e * n_vert + j, per)
         src = pl.multiple_of(((part ^ chip % plane) * per + place) * BLK, BLK)
         rows = slice((n_slash + j) * BLK, (n_slash + j + 1) * BLK)
         kg[rows, :HD] = kv_vert[pl.ds(src, BLK), :HD]
-        vg[rows, :HD] = kv_vert[pl.ds(src, BLK), HD:]
-    vg[:, HD:] = jnp.ones((width, HD), vg.dtype)
+        for vg in vgs:
+            vg[rows, :HD] = kv_vert[pl.ds(src, BLK), HD:]
+    for vg in vgs:
+        vg[:, HD:] = ones
     row = lax.broadcasted_iota(jnp.int32, (BLK, HD), 0)
     col = lax.broadcasted_iota(jnp.int32, (BLK, HD), 1)
     eye = jnp.where(row == col, 1.0, 0.0).astype(qx.dtype)
-    for g in range(group):
-        qx[g * BLK : (g + 1) * BLK, HD:] = eye
-
-    for slot in range(pair):
-
-        def one_block(b, carry, slot=slot):
-            rel = (core ^ slot if pair > 1 else 0) * local + b
-            here = chip * chip_blocks + rel
-            starts = [here - slash[e, j] for j in range(n_slash)]
-            for j in range(n_slash):
-                off = slash[e, j]
-                src = pl.multiple_of((reach * chip_blocks + rel - off) * BLK, BLK)
-                rows = slice(j * BLK, (j + 1) * BLK)
-                kg[rows, :HD] = win[pl.ds(src, BLK), :HD]
-                vg[rows, :HD] = win[pl.ds(src, BLK), HD:]
-                kind = jnp.where(starts[j] < 0, 2, jnp.where(off == 0, 1, 0))
-                kg[rows, HD:] = masks[kind]
-            for j in range(n_vert):
-                block = vert[e, j]
-                hidden = block >= here
-                for start in starts:
-                    hidden = hidden | (block == start)
-                rows = slice((n_slash + j) * BLK, (n_slash + j + 1) * BLK)
-                kg[rows, HD:] = masks[jnp.where(hidden, 2, 0)]
-            q_rows = pl.ds(pl.multiple_of(b * BLK, BLK), BLK)
-            for g in range(group):
-                qx[g * BLK : (g + 1) * BLK, :HD] = q_refs[slot][q_rows, g * HD : (g + 1) * HD]
-            top = None
-            for t in range(0, width, step):
-                s = lax.dot_general(
-                    qx[...], kg[t : t + step, :], (((1,), (1,)), ((), ())),
-                    preferred_element_type=jnp.float32,
-                )
-                sc[:, t : t + step] = s
-                for u in range(0, step, HD):
-                    piece = s[:, u : u + HD]
-                    top = piece if top is None else jnp.maximum(top, piece)
-            top = jnp.max(top, axis=1, keepdims=True)
-            acc = None
-            for t in range(0, width, step):
-                p = jnp.exp2((sc[:, t : t + step] - top) * factor).astype(vg.dtype)
-                o = jnp.dot(p, vg[t : t + step, :], preferred_element_type=jnp.float32)
-                acc = o if acc is None else acc + o
-            res = (acc[:, :HD] / acc[:, HD:]).astype(out_refs[slot].dtype)
-            for g in range(group):
-                out_refs[slot][q_rows, g * HD : (g + 1) * HD] = res[g * BLK : (g + 1) * BLK]
-            return carry
-
-        lax.fori_loop(0, local, one_block, 0)
+    for i in range(chip_blocks):
+        slot, b = divmod(i, local)
+        for g in range(group):
+            rows = slice(g * BLK, (g + 1) * BLK)
+            qx[i, rows, :HD] = q_refs[slot][b * BLK : (b + 1) * BLK, g * HD : (g + 1) * HD]
+            qx[i, rows, HD:] = eye
+
+    def within(i):
+        return (core ^ i // local) * local + i % local if pair > 1 else i
+
+    def take(i, j):
+        src = (reach * chip_blocks + within(i) - slash[e, j]) * BLK
+        return pl.ds(pl.multiple_of(src, BLK), BLK)
+
+    def place_keys(i):
+        here = chip * chip_blocks + within(i)
+        starts = [here - slash[e, j] for j in range(n_slash)]
+        for j in range(n_slash):
+            rows = slice(j * BLK, (j + 1) * BLK)
+            kg[rows, :HD] = win[take(i, j), :HD]
+            kind = jnp.where(starts[j] < 0, 2, jnp.where(slash[e, j] == 0, 1, 0))
+            kg[rows, HD:] = masks[kind]
+        for j in range(n_vert):
+            block = vert[e, j]
+            hidden = block >= here
+            for start in starts:
+                hidden = hidden | (block == start)
+            rows = slice((n_slash + j) * BLK, (n_slash + j + 1) * BLK)
+            kg[rows, HD:] = masks[jnp.where(hidden, 2, 0)]
+
+    def place_values(i, at):
+        for j in range(n_slash):
+            vgs[at][j * BLK : (j + 1) * BLK, :HD] = win[take(i, j), HD:]
+
+    def score_tile(i, at, t):
+        s = lax.dot_general(
+            qx[i], kg[t : t + step, :], (((1,), (1,)), ((), ())),
+            preferred_element_type=jnp.float32,
+        )
+        scs[at][:, t : t + step] = s
+        top = s[:, :HD]
+        for u in range(HD, step, HD):
+            top = jnp.maximum(top, s[:, u : u + HD])
+        tops[at][...] = top if t == 0 else jnp.maximum(tops[at][...], top)
+
+    def soften(at, r, some):
+        rows = slice(r, r + some)
+        top = jnp.max(tops[at][rows, :], axis=1, keepdims=True)
+        for t in range(0, width, step):
+            p = jnp.exp2((scs[at][rows, t : t + step] - top) * factor)
+            ps[at][rows, t : t + step] = p.astype(ps[at].dtype)
+
+    def weigh(i, at):
+        acc = jnp.dot(ps[at][...], vgs[at][...], preferred_element_type=jnp.float32)
+        res[i] = (acc[:, :HD] / acc[:, HD:]).astype(res.dtype)
+
+    n_tiles = width // step
+    some = group * BLK // n_tiles
+
+    def stage(i, at, ahead, behind):
+        place_values(i, at)
+        if ahead:
+            place_keys(i + 1)
+        if behind:
+            weigh(i - 1, 1 - at)
+        for u in range(n_tiles):
+            if ahead:
+                score_tile(i + 1, 1 - at, u * step)
+            soften(at, u * some, some)
+
+    place_keys(0)
+    for u in range(n_tiles):
+        score_tile(0, 0, u * step)
+    stage(0, 0, chip_blocks > 1, False)
+
+    def two_blocks(n, carry):
+        stage(2 * n + 1, 1, True, True)
+        stage(2 * n + 2, 0, True, True)
+        return carry
+
+    inner = max(chip_blocks - 2, 0) // 2
+    lax.fori_loop(0, inner, two_blocks, 0)
+    for i in range(2 * inner + 1, chip_blocks):
+        stage(i, i % 2, i + 1 < chip_blocks, True)
+    weigh(chip_blocks - 1, (chip_blocks - 1) % 2)
+    for i in range(chip_blocks):
+        slot, b = divmod(i, local)
+        for g in range(group):
+            out_refs[slot][b * BLK : (b + 1) * BLK, g * HD : (g + 1) * HD] = res[
+                i, g * BLK : (g + 1) * BLK
+            ]
 
 
 def attend(e, queries, q_other, windows, kv_vert, masks, vert, slash, info, local, plane):
@@ -177,7 +223,8 @@
     width = (n_slash + n_vert) * BLK
     win_rows = sum(w.shape[0] for w in windows)
     dtype = queries.dtype
-    rows = pair * local * group * BLK
+    blocks = pair * local
+    rows = blocks * group * BLK
     q_specs = [pl.BlockSpec((dev_rows, wide), lambda i, info, *_: (0, info[1] * heads + e))]
     if pair > 1:
         q_specs.append(pl.BlockSpec((dev_rows, wide), lambda i, *_: (0, e)))
@@ -197,10 +244,13 @@
             scratch_shapes=[
                 pltpu.VMEM((win_rows, 2 * HD), dtype),
                 pltpu.VMEM((width, 2 * HD), dtype),
-                pltpu.VMEM((width, 2 * HD), dtype),
-                pltpu.VMEM((group * BLK, 2 * HD), dtype),
-                pltpu.VMEM((group * BLK, width), jnp.float32),
-            ],
+                pltpu.VMEM((blocks, group * BLK, 2 * HD), dtype),
+                pltpu.VMEM((blocks, group * BLK, HD), dtype),
+            ]
+            + [pltpu.VMEM((width, 2 * HD), dtype)] * 2
+            + [pltpu.VMEM((group * BLK, width), jnp.float32)] * 2
+            + [pltpu.VMEM((group * BLK, HD), jnp.float32)] * 2
+            + [pltpu.VMEM((group * BLK, width), dtype)] * 2,
         ),
         out_shape=[jax.ShapeDtypeStruct((dev_rows, wide), dtype)] * pair,
         compiler_params=pltpu.CompilerParams(vmem_limit_bytes=VMEM_LIMIT),

time: 296 us -> 275 us (0.929)
  Pallas kernels: 136 us -> 111 us
  starting transfers between devices: 58.3 us -> 61.5 us
    pallas_call x4, Pallas kernels: 97.5 us -> 72.9 us  [attend(): pl.pallas_call(functools.partial(attend_kernel, (e, pair, local, group, r...]
    ppermute x16, starting transfers between devices: 47.7 us -> 51 us  [crossed(): return lax.ppermute(value, 'ctx', [(i, i ^ bits) for i in range(size)])]
  transfers between devices with their start and end apart: 22 -> 22, of which waited for: 11 -> 11; matrix products, arithmetic and copies ran while one was open for 3% -> 4% of each run, Pallas kernels for 40% -> 34%
where the time goes in v3:
time: 275 us; the launch traced here: 274 us
  Pallas kernels  111 us (40%)
  waiting for transfers between devices  83.6 us (30%)
  starting transfers between devices  61.5 us (22%)
  local copies, waits for them, and re-layouts  10.4 us (4%)
  other arithmetic  7.01 us (3%)
    pallas_call x4, Pallas kernels, attend(): pl.pallas_call(functools.partial(attend_kernel, (e, pair, local, group, r...  72.9 us
    ppermute x16, starting transfers between devices, crossed(): return lax.ppermute(value, 'ctx', [(i, i ^ bits) for i in range(size)])  51 us
    ppermute x16, waiting for transfers between devices, crossed(): return lax.ppermute(value, 'ctx', [(i, i ^ bits) for i in range(size)])  47.6 us
    ppermute x6, waiting for transfers between devices, shifted(): return lax.ppermute(value, 'ctx', [(i, i + by) for i in range(size - by)])  36.1 us
    pallas_call x2, Pallas kernels, project(): pl.pallas_call(functools.partial(project_kernel, n, before is not None),...  33.8 us
    ppermute x6, starting transfers between devices, shifted(): return lax.ppermute(value, 'ctx', [(i, i + by) for i in range(size - by)])  10.4 us
    unnamed x36, local copies, waits for them, and re-layouts  6.14 us
  transfers between devices with their start and end apart: 22, of which 11 were waited for; matrix products, arithmetic and copies ran while one was open for 4% of the time, Pallas kernels for 34%

profile of v3, /device:TPU:25, one launch (start us, length us, event | category | flops | bytes accessed | tf_op | source)
XLA Modules:
  0.0 273.9 jit_solution(6752049659630592756)
XLA Ops:
  5.4 4.5 %prepare.1 = (bf16[1024,256]{1,0:T(8,128)(2,1)}, bf16[1024,256]{1,0:T(8,128)(2,1)}, bf16[1024,256]{1,0:T(8,128)(2,1)}, bf16[1024,256]{1,0:T(8,128)(2,1)}, bf16[1...) custom-call(s32[2]{0:T(128)} %pad_add_fusion.info, ...), custom_call_target="tpu_custom_call" | custom-call | bytes 8388608 | tf_op jit(solution)/shard_map/prepare/pallas_call | solution.py:73
  12.6 1.7 constant_dynamic-slice_fusion.2
  15.7 7.6 %collective-permute-done.4 = bf16[1024,256]{1,0:T(8,128)(2,1)S(1)} collective-permute-done((bf16[1024,256]{1,0:T(8,128)(2,1)}, bf16[1024,256]{1,0:T(8,128)(2,1)S(1)}, u32[]{:S(2)}, u32[]{:S(2)}) %collective-permute-start.4) | collective-permute-done | bytes 524320 | tf_op jit(solution)/shard_map/ppermute | solution.py:26
  24.2 11.3 %collective-permute-done.6 = bf16[1024,256]{1,0:T(8,128)(2,1)} collective-permute-done((bf16[1024,256]{1,0:T(8,128)(2,1)}, bf16[1024,256]{1,0:T(8,128)(2,1)}, u32[]{:S(2)}, u32[]{:S(2)}) %collective-permute-start.6) | collective-permute-done | bytes 524320 | tf_op jit(solution)/shard_map/ppermute | solution.py:26
  38.4 2.1 collective-permute-start.2
  40.5 1.9 collective-permute-start.13
  43.9 1.9 collective-permute-start.15
  45.8 5.1 %collective-permute-done.7 = bf16[1024,256]{1,0:T(8,128)(2,1)S(1)} collective-permute-done((bf16[1024,256]{1,0:T(8,128)(2,1)S(1)}, bf16[1024,256]{1,0:T(8,128)(2,1)S(1)}, u32[]{:S(2)}, u32[]{:S(2)}) %collective-permute-start.7) | collective-permute-done | bytes 524320 | tf_op jit(solution)/shard_map/ppermute | solution.py:21
  50.8 1.9 collective-permute-start.17
  52.9 8.2 %collective-permute-done.2.refs_4_ = bf16[1024,256]{1,0:T(8,128)(2,1)} collective-permute-done((bf16[1024,256]{1,0:T(8,128)(2,1)}, bf16[1024,256]{1,0:T(8,128)(2,1)}, u32[]{:S(2)}, u32[]{:S(2)}) %collective-permute-start.2) | collective-permute-done | bytes 524320 | tf_op jit(solution)/shard_map/ppermute | solution.py:21
  63.5 8.8 %collective-permute-done.13.refs_4_ = bf16[1024,256]{1,0:T(8,128)(2,1)} collective-permute-done((bf16[1024,256]{1,0:T(8,128)(2,1)}, bf16[1024,256]{1,0:T(8,128)(2,1)}, u32[]{:S(2)}, u32[]{:S(2)}) %collective-permute-start.13) | collective-permute-done | bytes 524320 | tf_op jit(solution)/shard_map/ppermute | solution.py:21
  73.5 14.0 %collective-permute-done.8 = bf16[1024,256]{1,0:T(8,128)(2,1)S(1)} collective-permute-done((bf16[1024,256]{1,0:T(8,128)(2,1)S(1)}, bf16[1024,256]{1,0:T(8,128)(2,1)S(1)}, u32[]{:S(2)}, u32[]{:S(2)}) %collective-permute-start.8) | collective-permute-done | bytes 524320 | tf_op jit(solution)/shard_map/ppermute | solution.py:21
  87.6 31.9 %collective-permute-start.11 = (bf16[1024,256]{1,0:T(8,128)(2,1)S(1)}, bf16[1024,256]{1,0:T(8,128)(2,1)S(1)}, u32[]{:S(2)}, u32[]{:S(2)}) collective-permute-start(bf16[1024,256]{1,0:T(8,128)(2,1)S(1)} %add.46), channel_id=1, source_target_pairs={{0,6},{1,7},{2,4},{3,5},{4,2},{5,3},{6,0},{7,1},{8,14},{9,15},{10,... | collective-permute-start | bytes 1572872 | tf_op jit(solution)/shard_map/ppermute | solution.py:26
  121.2 8.0 %collective-permute-done.11 = bf16[1024,256]{1,0:T(8,128)(2,1)S(1)} collective-permute-done((bf16[1024,256]{1,0:T(8,128)(2,1)S(1)}, bf16[1024,256]{1,0:T(8,128)(2,1)S(1)}, u32[]{:S(2)}, u32[]{:S(2)}) %collective-permute-start.11) | collective-permute-done | bytes 524320 | tf_op jit(solution)/shard_map/ppermute | solution.py:26
  129.2 13.8 %collective-permute-done.10 = bf16[1024,256]{1,0:T(8,128)(2,1)S(1)} collective-permute-done((bf16[1024,256]{1,0:T(8,128)(2,1)S(1)}, bf16[1024,256]{1,0:T(8,128)(2,1)S(1)}, u32[]{:S(2)}, u32[]{:S(2)}) %collective-permute-start.10) | collective-permute-done | bytes 524320 | tf_op jit(solution)/shard_map/ppermute | solution.py:26
  146.0 4.7 %collective-permute-done.14.refs_3_ = bf16[1024,256]{1,0:T(8,128)(2,1)S(1)} collective-permute-done((bf16[1024,256]{1,0:T(8,128)(2,1)S(1)}, bf16[1024,256]{1,0:T(8,128)(2,1)S(1)}, u32[]{:S(2)}, u32[]{:S(2)}) %collective-permute-start.14) | collective-permute-done | bytes 524320 | tf_op jit(solution)/shard_map/ppermute | solution.py:26
  151.5 18.3 %attend.5 = (bf16[512,512]{1,0:T(8,128)(2,1)}, bf16[512,512]{1,0:T(8,128)(2,1)}) custom-call(s32[2]{0:T(128)} %pad_add_fusion.info, s32[4,8]{1,0:T(4,128)} %constant_dynamic-slice_fusion.4.vert, s32[4,8]{1,0:T(4,128)} %constant_dynamic-slice_fusion.3.slash, bf16[512,4096]{1,0:T(8,128)(2,1)} %refs_0_.9, bf16[512,2048]{1,0:T(8,128)(2,1)} %collective-permute-done.refs_1_, ...), custom_call_target="tpu_custom_call" | custom-call | flops 8589934592 | bytes 3670016 | tf_op jit(solution)/shard_map/attend/pallas_call | solution.py:235
  169.8 7.4 %collective-permute-start.19 = (bf16[512,512]{1,0:T(8,128)(2,1)}, bf16[512,512]{1,0:T(8,128)(2,1)S(1)}, u32[]{:S(2)}, u32[]{:S(2)}) collective-permute-start(bf16[512,512]{1,0:T(8,128)(2,1)} %get-tuple-element.34), channel_id=1, source_target_pairs={{0,1},{1,0},{2,3},{3,2},{4,5},{5,4},{6,7},{7,6},{8,9},{9,8},{10,11... | collective-permute-start | bytes 1572872 | tf_op jit(solution)/shard_map/ppermute | solution.py:26
  178.0 18.3 %attend.6 = (bf16[512,512]{1,0:T(8,128)(2,1)}, bf16[512,512]{1,0:T(8,128)(2,1)}) custom-call(s32[2]{0:T(128)} %pad_add_fusion.info, s32[4,8]{1,0:T(4,128)} %constant_dynamic-slice_fusion.4.vert, s32[4,8]{1,0:T(4,128)} %constant_dynamic-slice_fusion.3.slash, bf16[512,4096]{1,0:T(8,128)(2,1)} %refs_0_.9, bf16[512,2048]{1,0:T(8,128)(2,1)} %collective-permute-done.refs_1_, ...), custom_call_target="tpu_custom_call" | custom-call | flops 8589934592 | bytes 3670016 | tf_op jit(solution)/shard_map/attend/pallas_call | solution.py:235
  196.3 3.3 %collective-permute-start.20 = (bf16[512,512]{1,0:T(8,128)(2,1)}, bf16[512,512]{1,0:T(8,128)(2,1)S(1)}, u32[]{:S(2)}, u32[]{:S(2)}) collective-permute-start(bf16[512,512]{1,0:T(8,128)(2,1)} %get-tuple-element.35), channel_id=1, source_target_pairs={{0,1},{1,0},{2,3},{3,2},{4,5},{5,4},{6,7},{7,6},{8,9},{9,8},{10,11... | collective-permute-start | bytes 1572872 | tf_op jit(solution)/shard_map/ppermute | solution.py:26
  200.5 18.0 %attend.7 = (bf16[512,512]{1,0:T(8,128)(2,1)}, bf16[512,512]{1,0:T(8,128)(2,1)}) custom-call(s32[2]{0:T(128)} %pad_add_fusion.info, s32[4,8]{1,0:T(4,128)} %constant_dynamic-slice_fusion.4.vert, s32[4,8]{1,0:T(4,128)} %constant_dynamic-slice_fusion.3.slash, bf16[512,4096]{1,0:T(8,128)(2,1)} %refs_0_.9, bf16[512,2048]{1,0:T(8,128)(2,1)} %collective-permute-done.refs_1_, ...), custom_call_target="tpu_custom_call" | custom-call | flops 8589934592 | bytes 3670016 | tf_op jit(solution)/shard_map/attend/pallas_call | solution.py:235
  219.3 18.3 %attend.4 = (bf16[512,512]{1,0:T(8,128)(2,1)}, bf16[512,512]{1,0:T(8,128)(2,1)}) custom-call(s32[2]{0:T(128)} %pad_add_fusion.info, s32[4,8]{1,0:T(4,128)} %constant_dynamic-slice_fusion.4.vert, s32[4,8]{1,0:T(4,128)} %constant_dynamic-slice_fusion.3.slash, bf16[512,4096]{1,0:T(8,128)(2,1)} %refs_0_.9, bf16[512,2048]{1,0:T(8,128)(2,1)} %collective-permute-done.refs_1_, ...), custom_call_target="tpu_custom_call" | custom-call | flops 8589934592 | bytes 3670016 | tf_op jit(solution)/shard_map/attend/pallas_call | solution.py:235
  239.2 20.8 %project.2.refs_4_ = f32[512,4096]{1,0:T(8,128)} custom-call(s32[2]{0:T(128)} %pad_add_fusion.info, bf16[512,512]{1,0:T(8,128)(2,1)} %get-tuple-element.29.refs_0_, bf16[512,512]{1,0:T(8,128)(2,1)} %get-tuple-element.31.refs_1_, bf16[512,512]{1,0:T(8,128)(2,1)} %get-tuple-element.33.refs_2_, bf16[512,512]{1,0:T(8,128)(2,1)} %copy-done.3, ...), custom_call_target="tpu_custom_call" | custom-call | flops 12884901888 | bytes 45088768 | tf_op jit(solution)/shard_map/project/pallas_call | solution.py:293
  260.9 13.0 %project.3 = bf16[512,4096]{1,0:T(8,128)(2,1)} custom-call(s32[2]{0:T(128)} %pad_add_fusion.info, bf16[512,512]{1,0:T(8,128)(2,1)} %get-tuple-element.26.refs_0_, bf16[512,512]{1,0:T(8,128)(2,1)} %copy-done.6, bf16[4096,4096]{1,0:T(8,128)(2,1)} %refs_3_.1, bf16[4096,4096]{1,0:T(8,128)(2,1)} %refs_3_.1, f32[512,4096]{1,0:T(8,128)} %project.2.refs_4_), custom_call_target="tpu_custom_call" | custom-call | flops 4294967296 | bytes 26214400 | tf_op jit(solution)/shard_map/project/pallas_call | solution.py:293
  (81 shorter events, 28.7 us)
Async XLA Ops:
  1.4 3.0 %collective-permute-start.1 = (bf16[512,1024]{1,0:T(8,128)(2,1)S(1)}, bf16[512,1024]{1,0:T(8,128)(2,1)S(1)}, u32[]{:S(2)}, u32[]{:S(2)}) collective-permute-start(bf16[512,1024]{1,0:T(8,128)(2,1)S(1)} %pad_maximum_fusion.1), channel_id=1, source_target_pairs={{0,1},{1,0},{2,3},{3,2},{4,5},{5,4},{6,7},{7,6},{8,9},{9,8},{10,11... | collective-permute-start | bytes 3145736 | tf_op jit(solution)/shard_map/ppermute | solution.py:26
  9.9 13.4 %collective-permute-start.4 = (bf16[1024,256]{1,0:T(8,128)(2,1)}, bf16[1024,256]{1,0:T(8,128)(2,1)S(1)}, u32[]{:S(2)}, u32[]{:S(2)}) collective-permute-start(bf16[1024,256]{1,0:T(8,128)(2,1)} %get-tuple-element.23), channel_id=1, source_target_pairs={{0,2},{1,3},{2,0},{3,1},{4,6},{5,7},{6,4},{7,5},{8,10},{9,11},{10,... | collective-permute-start | bytes 1572872 | tf_op jit(solution)/shard_map/ppermute | solution.py:26
  11.2 13.0 %collective-permute-start.5 = (bf16[1024,256]{1,0:T(8,128)(2,1)}, bf16[1024,256]{1,0:T(8,128)(2,1)}, u32[]{:S(2)}, u32[]{:S(2)}) collective-permute-start(bf16[1024,256]{1,0:T(8,128)(2,1)} %get-tuple-element.24), channel_id=1, source_target_pairs={{0,4},{1,5},{2,6},{3,7},{4,0},{5,1},{6,2},{7,3},{8,12},{9,13},{10,... | collective-permute-start | bytes 1572872 | tf_op jit(solution)/shard_map/ppermute | solution.py:26
  12.4 23.1 %collective-permute-start.6 = (bf16[1024,256]{1,0:T(8,128)(2,1)}, bf16[1024,256]{1,0:T(8,128)(2,1)}, u32[]{:S(2)}, u32[]{:S(2)}) collective-permute-start(bf16[1024,256]{1,0:T(8,128)(2,1)} %get-tuple-element.25), channel_id=1, source_target_pairs={{0,6},{1,7},{2,4},{3,5},{4,2},{5,3},{6,0},{7,1},{8,14},{9,15},{10,... | collective-permute-start | bytes 1572872 | tf_op jit(solution)/shard_map/ppermute | solution.py:26
  14.3 131.7 %collective-permute-start = (bf16[512,2048]{1,0:T(8,128)(2,1)S(1)}, bf16[512,2048]{1,0:T(8,128)(2,1)}, u32[]{:S(2)}, u32[]{:S(2)}) collective-permute-start(bf16[512,2048]{1,0:T(8,128)(2,1)S(1)} %constant_dynamic-slice_fusion.2), channel_id=1, source_target_pairs={{0,1},{1,0},{2,3},{3,2},{4,5},{5,4},{6,7},{7,6},{8,9},{9,8},{10,11... | collective-permute-start | bytes 6291464 | tf_op jit(solution)/shard_map/ppermute | solution.py:26
  37.1 13.8 %collective-permute-start.7 = (bf16[1024,256]{1,0:T(8,128)(2,1)S(1)}, bf16[1024,256]{1,0:T(8,128)(2,1)S(1)}, u32[]{:S(2)}, u32[]{:S(2)}) collective-permute-start(bf16[1024,256]{1,0:T(8,128)(2,1)S(1)} %add_add_fusion), channel_id=1, source_target_pairs={{0,8},{1,9},{2,10},{3,11},{4,12},{5,13},{6,14},{7,15},{8,16},{9,17... | collective-permute-start | bytes 1572872 | tf_op jit(solution)/shard_map/ppermute | solution.py:21
  38.4 22.8 %collective-permute-start.2 = (bf16[1024,256]{1,0:T(8,128)(2,1)}, bf16[1024,256]{1,0:T(8,128)(2,1)}, u32[]{:S(2)}, u32[]{:S(2)}) collective-permute-start(bf16[1024,256]{1,0:T(8,128)(2,1)} %get-tuple-element.21.refs_2_), channel_id=1, source_target_pairs={{0,4},{1,5},{2,6},{3,7},{4,8},{5,9},{6,10},{7,11},{8,12},{9,13},{1... | collective-permute-start | bytes 1572872 | tf_op jit(solution)/shard_map/ppermute | solution.py:21
  40.5 31.8 %collective-permute-start.13 = (bf16[1024,256]{1,0:T(8,128)(2,1)}, bf16[1024,256]{1,0:T(8,128)(2,1)}, u32[]{:S(2)}, u32[]{:S(2)}) collective-permute-start(bf16[1024,256]{1,0:T(8,128)(2,1)} %get-tuple-element.28.refs_2_), channel_id=1, source_target_pairs={{0,4},{1,5},{2,6},{3,7},{4,8},{5,9},{6,10},{7,11},{8,12},{9,13},{1... | collective-permute-start | bytes 1572872 | tf_op jit(solution)/shard_map/ppermute | solution.py:21
  43.1 76.8 %copy-start.10 = (bf16[1024,256]{1,0:T(8,128)(2,1)S(1)}, bf16[1024,256]{1,0:T(8,128)(2,1)}, u32[]{:S(2)}) copy-start(bf16[1024,256]{1,0:T(8,128)(2,1)} %get-tuple-element.30.refs_2_) | copy-start | bytes 1572868
  43.1 78.1 %copy-start.9 = (bf16[1024,256]{1,0:T(8,128)(2,1)S(1)}, bf16[1024,256]{1,0:T(8,128)(2,1)}, u32[]{:S(2)}) copy-start(bf16[1024,256]{1,0:T(8,128)(2,1)} %get-tuple-element.32.refs_2_) | copy-start | bytes 1572868
  43.9 75.6 %collective-permute-start.15 = (bf16[1024,256]{1,0:T(8,128)(2,1)}, bf16[1024,256]{1,0:T(8,128)(2,1)S(1)}, u32[]{:S(2)}, u32[]{:S(2)}) collective-permute-start(bf16[1024,256]{1,0:T(8,128)(2,1)} %get-tuple-element.30.refs_2_), channel_id=1, source_target_pairs={{0,4},{1,5},{2,6},{3,7},{4,8},{5,9},{6,10},{7,11},{8,12},{9,13},{1... | collective-permute-start | bytes 1572872 | tf_op jit(solution)/shard_map/ppermute | solution.py:21
  50.8 69.1 %collective-permute-start.17 = (bf16[1024,256]{1,0:T(8,128)(2,1)}, bf16[1024,256]{1,0:T(8,128)(2,1)S(1)}, u32[]{:S(2)}, u32[]{:S(2)}) collective-permute-start(bf16[1024,256]{1,0:T(8,128)(2,1)} %get-tuple-element.32.refs_2_), channel_id=1, source_target_pairs={{0,4},{1,5},{2,6},{3,7},{4,8},{5,9},{6,10},{7,11},{8,12},{9,13},{1... | collective-permute-start | bytes 1572872 | tf_op jit(solution)/shard_map/ppermute | solution.py:21
  61.1 26.3 %collective-permute-start.8 = (bf16[1024,256]{1,0:T(8,128)(2,1)S(1)}, bf16[1024,256]{1,0:T(8,128)(2,1)S(1)}, u32[]{:S(2)}, u32[]{:S(2)}) collective-permute-start(bf16[1024,256]{1,0:T(8,128)(2,1)S(1)} %add.45), channel_id=1, source_target_pairs={{0,16},{1,17},{2,18},{3,19},{4,20},{5,21},{6,22},{7,23},{8,24},{9,... | collective-permute-start | bytes 1572872 | tf_op jit(solution)/shard_map/ppermute | solution.py:21
  87.6 41.7 %collective-permute-start.11 = (bf16[1024,256]{1,0:T(8,128)(2,1)S(1)}, bf16[1024,256]{1,0:T(8,128)(2,1)S(1)}, u32[]{:S(2)}, u32[]{:S(2)}) collective-permute-start(bf16[1024,256]{1,0:T(8,128)(2,1)S(1)} %add.46), channel_id=1, source_target_pairs={{0,6},{1,7},{2,4},{3,5},{4,2},{5,3},{6,0},{7,1},{8,14},{9,15},{10,... | collective-permute-start | bytes 1572872 | tf_op jit(solution)/shard_map/ppermute | solution.py:26
  119.5 23.6 %collective-permute-start.10 = (bf16[1024,256]{1,0:T(8,128)(2,1)S(1)}, bf16[1024,256]{1,0:T(8,128)(2,1)S(1)}, u32[]{:S(2)}, u32[]{:S(2)}) collective-permute-start(bf16[1024,256]{1,0:T(8,128)(2,1)S(1)} %add.46), channel_id=1, source_target_pairs={{0,4},{1,5},{2,6},{3,7},{4,0},{5,1},{6,2},{7,3},{8,12},{9,13},{10,... | collective-permute-start | bytes 1572872 | tf_op jit(solution)/shard_map/ppermute | solution.py:26
  119.5 23.6 %collective-permute-start.9 = (bf16[1024,256]{1,0:T(8,128)(2,1)S(1)}, bf16[1024,256]{1,0:T(8,128)(2,1)S(1)}, u32[]{:S(2)}, u32[]{:S(2)}) collective-permute-start(bf16[1024,256]{1,0:T(8,128)(2,1)S(1)} %add.46), channel_id=1, source_target_pairs={{0,2},{1,3},{2,0},{3,1},{4,6},{5,7},{6,4},{7,5},{8,10},{9,11},{10,... | collective-permute-start | bytes 1572872 | tf_op jit(solution)/shard_map/ppermute | solution.py:26
  119.9 30.8 %collective-permute-start.14 = (bf16[1024,256]{1,0:T(8,128)(2,1)S(1)}, bf16[1024,256]{1,0:T(8,128)(2,1)S(1)}, u32[]{:S(2)}, u32[]{:S(2)}) collective-permute-start(bf16[1024,256]{1,0:T(8,128)(2,1)S(1)} %broadcast_select_fusion.2), channel_id=1, source_target_pairs={{0,2},{1,3},{2,0},{3,1},{4,6},{5,7},{6,4},{7,5},{8,10},{9,11},{10,... | collective-permute-start | bytes 1572872 | tf_op jit(solution)/shard_map/ppermute | solution.py:26
  129.2 89.3 %collective-permute-start.3 = (bf16[1024,256]{1,0:T(8,128)(2,1)S(1)}, bf16[1024,256]{1,0:T(8,128)(2,1)S(1)}, u32[]{:S(2)}, u32[]{:S(2)}) collective-permute-start(bf16[1024,256]{1,0:T(8,128)(2,1)S(1)} %broadcast_select_fusion.3), channel_id=1, source_target_pairs={{0,2},{1,3},{2,0},{3,1},{4,6},{5,7},{6,4},{7,5},{8,10},{9,11},{10,... | collective-permute-start | bytes 1572872 | tf_op jit(solution)/shard_map/ppermute | solution.py:26
  143.1 34.1 %collective-permute-start.16 = (bf16[1024,256]{1,0:T(8,128)(2,1)S(1)}, bf16[1024,256]{1,0:T(8,128)(2,1)S(1)}, u32[]{:S(2)}, u32[]{:S(2)}) collective-permute-start(bf16[1024,256]{1,0:T(8,128)(2,1)S(1)} %broadcast_select_fusion.1), channel_id=1, source_target_pairs={{0,2},{1,3},{2,0},{3,1},{4,6},{5,7},{6,4},{7,5},{8,10},{9,11},{10,... | collective-permute-start | bytes 1572872 | tf_op jit(solution)/shard_map/ppermute | solution.py:26
  143.1 56.6 %collective-permute-start.18 = (bf16[1024,256]{1,0:T(8,128)(2,1)S(1)}, bf16[1024,256]{1,0:T(8,128)(2,1)S(1)}, u32[]{:S(2)}, u32[]{:S(2)}) collective-permute-start(bf16[1024,256]{1,0:T(8,128)(2,1)S(1)} %broadcast_select_fusion), channel_id=1, source_target_pairs={{0,2},{1,3},{2,0},{3,1},{4,6},{5,7},{6,4},{7,5},{8,10},{9,11},{10,... | collective-permute-start | bytes 1572872 | tf_op jit(solution)/shard_map/ppermute | solution.py:26
  169.8 68.3 %collective-permute-start.19 = (bf16[512,512]{1,0:T(8,128)(2,1)}, bf16[512,512]{1,0:T(8,128)(2,1)S(1)}, u32[]{:S(2)}, u32[]{:S(2)}) collective-permute-start(bf16[512,512]{1,0:T(8,128)(2,1)} %get-tuple-element.34), channel_id=1, source_target_pairs={{0,1},{1,0},{2,3},{3,2},{4,5},{5,4},{6,7},{7,6},{8,9},{9,8},{10,11... | collective-permute-start | bytes 1572872 | tf_op jit(solution)/shard_map/ppermute | solution.py:26
  196.3 41.8 %collective-permute-start.20 = (bf16[512,512]{1,0:T(8,128)(2,1)}, bf16[512,512]{1,0:T(8,128)(2,1)S(1)}, u32[]{:S(2)}, u32[]{:S(2)}) collective-permute-start(bf16[512,512]{1,0:T(8,128)(2,1)} %get-tuple-element.35), channel_id=1, source_target_pairs={{0,1},{1,0},{2,3},{3,2},{4,5},{5,4},{6,7},{7,6},{8,9},{9,8},{10,11... | collective-permute-start | bytes 1572872 | tf_op jit(solution)/shard_map/ppermute | solution.py:26
  218.5 19.6 %collective-permute-start.21 = (bf16[512,512]{1,0:T(8,128)(2,1)}, bf16[512,512]{1,0:T(8,128)(2,1)S(1)}, u32[]{:S(2)}, u32[]{:S(2)}) collective-permute-start(bf16[512,512]{1,0:T(8,128)(2,1)} %get-tuple-element.36), channel_id=1, source_target_pairs={{0,1},{1,0},{2,3},{3,2},{4,5},{5,4},{6,7},{7,6},{8,9},{9,8},{10,11... | collective-permute-start | bytes 1572872 | tf_op jit(solution)/shard_map/ppermute | solution.py:26
  237.6 22.4 %collective-permute-start.12 = (bf16[512,512]{1,0:T(8,128)(2,1)}, bf16[512,512]{1,0:T(8,128)(2,1)S(1)}, u32[]{:S(2)}, u32[]{:S(2)}) collective-permute-start(bf16[512,512]{1,0:T(8,128)(2,1)} %get-tuple-element.27), channel_id=1, source_target_pairs={{0,1},{1,0},{2,3},{3,2},{4,5},{5,4},{6,7},{7,6},{8,9},{9,8},{10,11... | collective-permute-start | bytes 1572872 | tf_op jit(solution)/shard_map/ppermute | solution.py:26
  (16 other events, 194.4 us)
